TPU v7x, 32 devices: a whole 2x2x4 slice. The times are simulated.
32 devices in a mesh: groups: 2 (over y), neuron: 16 (over z, x, core).
Axes of the slice: x: 2, y: 2, z: 4, core: 2. Of those that a mesh axis runs over, the one named last changes fastest.
Arguments:
- tokens: bfloat16 [512, 12288], P(('groups', 'neuron')), parts along dimension 0, may hold values from -6 to 6
- active: int32 [128, 3], P(('groups', 'neuron')), parts along dimension 0, may hold values from 0 to 31, as said below
- ln_gain: bfloat16 [12288], replicated, may hold values from 0.099609375 to 1.8984375
- ln_bias: bfloat16 [12288], replicated, may hold values from -3 to 3
- w_in: bfloat16 [12288, 4096], P(None, 'neuron'), may hold values from -0.0546875 to 0.0546875
- b_in: bfloat16 [4096], P('neuron'), may hold values from -3 to 3
- w_out: bfloat16 [4096, 12288], P('neuron'), may hold values from -0.3125 to 0.3125
- b_out: bfloat16 [12288], replicated, may hold values from -2 to 2
Outputs:
- mixed: bfloat16 [512, 12288], P(('groups', 'neuron')), parts along dimension 0
There are 2 independent parts, one for each index of `groups`. A program takes and returns all parts, laid end to end along the dimension named above; an argument that names none is the same for every part. Nothing has to cross between parts.
Inputs may be any that keep to these rules, and one draw needn't show every extreme that they name: Each row names 3 distinct blocks. Block b lies with device b // 2 of the neuron axis, and the 4 requests held by one device never have active blocks lying with the same device.
All inputs are finite; a program needn't handle non-finite values.
Results may differ from a plain program's by a relative error of at most 0.0051.
Values may be sent and summed in bfloat16 or wider, within the bound.
No kernel may reach another device: no remote copies, remote signals or barrier semaphores. Data moves between devices by JAX's collectives and lax.ppermute only.
A program may use at most 128 MiB of HBM per device.

v0:
```python
import jax
import jax.numpy as jnp
from jax import lax
from jax.sharding import PartitionSpec as P

BLK = 128


epsilon = 1e-05


def layer_norm(tokens, ln_gain, ln_bias):
    widened = tokens.astype(jnp.float32)
    row_mean = jnp.mean(widened, axis=1, keepdims=True)
    centred = widened - row_mean
    row_var = jnp.mean(centred * centred, axis=1, keepdims=True)
    scaled = centred * lax.rsqrt(row_var + epsilon)
    return (scaled * ln_gain.astype(jnp.float32) + ln_bias.astype(jnp.float32)).astype(jnp.bfloat16)


def body(tokens, active, ln_gain, ln_bias, w_in, b_in, w_out, b_out):
    req_count = active.shape[0]
    node_count = tokens.shape[0] // req_count
    feature_count = tokens.shape[1]
    device_count = lax.axis_size("neuron")
    per_device = w_in.shape[1] // BLK
    normed = layer_norm(tokens, ln_gain, ln_bias)
    by_request = normed.reshape(req_count, node_count, feature_count)
    block_ids = jnp.arange(device_count * per_device, dtype=jnp.int32)
    opened = jnp.sum((active[:, :, None] == block_ids[None, None, :]).astype(jnp.int32), axis=1)
    opened = opened.reshape(req_count, device_count, per_device)
    touched = jnp.max(opened, axis=2)
    chosen = jnp.sum(touched * jnp.arange(req_count, dtype=jnp.int32)[:, None], axis=0)
    outgoing = jnp.take(by_request, chosen, axis=0)
    outgoing_flags = jnp.broadcast_to(
        jnp.sum(opened, axis=0)[:, None, :], (device_count, node_count, per_device)
    )
    bias_wide = b_in.astype(jnp.float32)
    slot_rows = lax.all_to_all(outgoing, "neuron", split_axis=0, concat_axis=0, tiled=True)
    slot_flags = lax.all_to_all(outgoing_flags, "neuron", split_axis=0, concat_axis=0, tiled=True)
    item_count = slot_rows.shape[1]
    flat_rows = slot_rows.reshape(-1, feature_count)
    preact = jnp.dot(flat_rows, w_in, preferred_element_type=jnp.float32) + bias_wide
    unit_mask = jnp.repeat(slot_flags.reshape(-1, per_device), BLK, axis=1).astype(jnp.float32)
    hidden = (jnp.maximum(preact, 0.0) * unit_mask).astype(jnp.bfloat16)
    partial_value = jnp.dot(hidden, w_out, preferred_element_type=jnp.float32).astype(jnp.bfloat16)
    partial_value = partial_value.reshape(device_count, item_count, feature_count)
    returned = lax.all_to_all(partial_value, "neuron", split_axis=0, concat_axis=0, tiled=True)
    selector = jnp.transpose(touched).astype(jnp.bfloat16)
    summed = jnp.einsum("pj,pnd->jnd", selector, returned, preferred_element_type=jnp.float32)
    mixed = (
        tokens.astype(jnp.float32) + summed.reshape(-1, feature_count) + b_out.astype(jnp.float32)
    )
    return mixed.astype(jnp.bfloat16)


def solution(mesh):
    placed = (
        P(("groups", "neuron"), None),
        P(("groups", "neuron"), None),
        P(),
        P(),
        P(None, "neuron"),
        P("neuron"),
        P("neuron", None),
        P(),
    )
    return jax.shard_map(
        body, mesh=mesh, in_specs=placed, out_specs=P(("groups", "neuron"), None), check_vma=False
    )
```

profile of v0, /device:TPU:15, one launch (start us, length us, event | category | flops | bytes accessed | tf_op | source)
XLA Modules:
  0.0 115.3 jit_solution(15870891697673911913)
XLA Ops:
  0.0 0.8 copy.28
  0.8 0.1 convert_reduce_fusion.1
  0.9 0.1 broadcast_in_dim.18
  0.9 0.7 broadcast_in_dim.19
  1.6 6.6 %all-to-all-start.1 = ((s32[16,4,2]{1,2,0:T(2,128)}), s32[16,4,2]{1,2,0:T(2,128)S(1)}, u32[]{:S(2)}, u32[]{:S(2)}) async-start(s32[16,4,2]{1,2,0:T(2,128)} %broadcast_in_dim.19), calls=%async_computation.1 | async-start | bytes 32768 | tf_op jit(solution)/shard_map/all_to_all | solution.py:40
  8.2 0.1 copy.29
  8.3 0.1 fusion.20
  8.5 1.2 %convert_reduce_fusion = f32[16]{0:T(128)S(1)} fusion(bf16[16,12288]{1,0:T(8,128)(2,1)} %param.8), kind=kLoop, calls=%fused_computation.7 | loop fusion | flops 393200 | bytes 393280 | tf_op jit(solution)/shard_map/reduce_sum | solution.py:14
  9.7 1.3 %fusion.7 = f32[16]{0:T(128)S(1)} fusion(bf16[16,12288]{1,0:T(8,128)(2,1)} %param.8, f32[16]{0:T(128)S(1)} %broadcast_multiply_fusion), kind=kLoop, calls=%fused_computation.14 | loop fusion | flops 786416 | bytes 393344 | tf_op jit(solution)/shard_map/reduce_sum | solution.py:16
  11.0 0.8 convert_element_type.48
  11.7 0.7 convert_element_type.49
  12.5 1.2 %fusion.10 = bf16[16,12288]{1,0:T(8,128)(2,1)S(1)} fusion(bf16[16,12288]{1,0:T(8,128)(2,1)} %param.8, f32[12288]{0:T(1024)S(1)} %convert_element_type.49, f32[12288]{0:T(1024)S(1)} %convert_element_type.48, f32[16]{0:T(128)S(1)} %add_rsqrt_fusion, f32[16]{0:T(128)S(1)} %broadcast_multiply_fusion), kind=kLoop, calls=%fused_computation.17 | loop fusion | flops 1179648 | bytes 884864 | tf_op jit(solution)/shard_map/convert_element_type | solution.py:18
  13.7 0.1 reshape.58
  13.8 1.9 %gather_fusion = bf16[16,4,12288]{2,1,0:T(4,128)(2,1)S(1)} fusion(bf16[4,4,12288]{2,1,0:T(4,128)(2,1)S(1)} %reshape.58, s32[1024]{0:T(1024)S(1)} %pad_clamp_fusion), kind=kCustom, calls=%fused_computation | custom fusion | bytes 3145792 | tf_op jit(solution)/shard_map/jit(_take)/gather | solution.py:34
  15.7 1.9 %broadcast_select_fusion = bf16[16,4,12288]{2,1,0:T(4,128)(2,1)} fusion(bf16[16,4,12288]{2,1,0:T(4,128)(2,1)S(1)} %gather_fusion, pred[16]{0:T(512)(128)(4,1)S(1)} %compare_and_fusion), kind=kLoop, calls=%fused_computation.4 | loop fusion | flops 786432 | bytes 3145744 | tf_op jit(solution)/shard_map/jit(_take)/select_n | solution.py:34
  17.7 0.0 all-to-all-done.1
  17.7 6.2 %all-to-all-start = ((bf16[16,4,12288]{2,1,0:T(4,128)(2,1)}), bf16[16,4,12288]{2,1,0:T(4,128)(2,1)S(1)}, u32[]{:S(2)}, u32[]{:S(2)}) async-start(bf16[16,4,12288]{2,1,0:T(4,128)(2,1)} %broadcast_select_fusion), calls=%async_computation | async-start | bytes 3145728 | tf_op jit(solution)/shard_map/all_to_all | solution.py:39
  23.8 0.1 copy.31
  23.9 0.1 copy.36
  24.0 36.0 %all-to-all-done = bf16[16,4,12288]{2,1,0:T(4,128)(2,1)S(1)} async-done(((bf16[16,4,12288]{2,1,0:T(4,128)(2,1)}), bf16[16,4,12288]{2,1,0:T(4,128)(2,1)S(1)}, u32[]{:S(2)}, u32[]{:S(2)}) %all-to-all-start) | async-done | bytes 1572896 | tf_op jit(solution)/shard_map/all_to_all | solution.py:39
  60.0 0.4 reshape.59
  60.4 0.1 broadcast_in_dim.34
  60.5 8.4 %convolution_convert_fusion = bf16[64,12288]{1,0:T(8,128)(2,1)S(1)} fusion(bf16[256,12288]{1,0:T(8,128)(2,1)} %param.14, bf16[64,12288]{1,0:T(8,128)(2,1)S(1)} %reshape.59, bf16[12288,256]{1,0:T(8,128)(2,1)} %param.12, f32[8,8,2,128]{3,2,1,0:T(2,128)S(1)} %bitcast.18, f32[256]{0:T(256)S(1)} %convert_element_type.51), kind=kOutput, calls=%fused_computation.1 | convolution fusion | flops 806158336 | bytes 15795200 | tf_op jit(solution)/shard_map/dot_general | solution.py:46
  68.9 1.5 %reshape.60 = bf16[16,4,12288]{2,1,0:T(4,128)(2,1)} reshape(bf16[64,12288]{1,0:T(8,128)(2,1)S(1)} %convolution_convert_fusion) | data formatting | bytes 3145728 | tf_op jit(solution)/shard_map/reshape | solution.py:47
  70.4 5.0 %all-to-all-start.2 = ((bf16[16,4,12288]{2,1,0:T(4,128)(2,1)}), bf16[16,4,12288]{2,1,0:T(4,128)(2,1)S(1)}, u32[]{:S(2)}, u32[]{:S(2)}) async-start(bf16[16,4,12288]{2,1,0:T(4,128)(2,1)} %reshape.60), calls=%async_computation.2 | async-start | bytes 3145728 | tf_op jit(solution)/shard_map/all_to_all | solution.py:48
  75.5 0.1 copy.39
  75.6 36.1 %all-to-all-done.2 = bf16[16,4,12288]{2,1,0:T(4,128)(2,1)S(1)} async-done(((bf16[16,4,12288]{2,1,0:T(4,128)(2,1)}), bf16[16,4,12288]{2,1,0:T(4,128)(2,1)S(1)}, u32[]{:S(2)}, u32[]{:S(2)}) %all-to-all-start.2) | async-done | bytes 1572896 | tf_op jit(solution)/shard_map/all_to_all | solution.py:48
  111.7 1.8 %fusion = f32[4,4,12288]{2,0,1:T(4,128)S(1)} fusion(bf16[16,4,12288]{2,1,0:T(4,128)(2,1)S(1)} %all-to-all-done.2, bf16[4,16]{1,0:T(4,128)(2,1)S(1)} %copy.39), kind=kOutput, calls=%fused_computation.2 | convolution fusion | flops 6291456 | bytes 2359424 | tf_op jit(solution)/shard_map/pj,pnd->jnd/dot_general | solution.py:50
  113.5 0.5 copy.35
  114.0 0.3 reshape.61
  114.2 0.2 copy-done
  114.4 0.8 fusion.12
  (14 shorter events, 0.1 us)
Async XLA Ops:
  1.6 16.0 %all-to-all-start.1 = ((s32[16,4,2]{1,2,0:T(2,128)}), s32[16,4,2]{1,2,0:T(2,128)S(1)}, u32[]{:S(2)}, u32[]{:S(2)}) async-start(s32[16,4,2]{1,2,0:T(2,128)} %broadcast_in_dim.19), calls=%async_computation.1 | async-start | bytes 32768 | tf_op jit(solution)/shard_map/all_to_all | solution.py:40
  17.7 6.2 %copy-start.2 = (bf16[256]{0:T(256)(128)(2,1)S(1)}, bf16[256]{0:T(256)(128)(2,1)}, u32[]{:S(2)}) copy-start(bf16[256]{0:T(256)(128)(2,1)} %param.13) | copy-start | bytes 1540
  17.7 42.3 %all-to-all-start = ((bf16[16,4,12288]{2,1,0:T(4,128)(2,1)}), bf16[16,4,12288]{2,1,0:T(4,128)(2,1)S(1)}, u32[]{:S(2)}, u32[]{:S(2)}) async-start(bf16[16,4,12288]{2,1,0:T(4,128)(2,1)} %broadcast_select_fusion), calls=%async_computation | async-start | bytes 3145728 | tf_op jit(solution)/shard_map/all_to_all | solution.py:39
  70.4 5.1 %copy-start.1 = (bf16[12288]{0:T(1024)(128)(2,1)S(1)}, bf16[12288]{0:T(1024)(128)(2,1)}, u32[]{:S(2)}) copy-start(bf16[12288]{0:T(1024)(128)(2,1)} %param.15) | copy-start | bytes 73732
  70.4 41.2 %all-to-all-start.2 = ((bf16[16,4,12288]{2,1,0:T(4,128)(2,1)}), bf16[16,4,12288]{2,1,0:T(4,128)(2,1)S(1)}, u32[]{:S(2)}, u32[]{:S(2)}) async-start(bf16[16,4,12288]{2,1,0:T(4,128)(2,1)} %reshape.60), calls=%async_computation.2 | async-start | bytes 3145728 | tf_op jit(solution)/shard_map/all_to_all | solution.py:48
  113.5 1.0 copy-start
where the time goes:
time: 116 us; the launch traced here: 115 us
  waiting for transfers between devices  72 us (62%)
  starting transfers between devices  17.7 us (15%)
  matrix products  10.2 us (9%)
  other arithmetic  8.23 us (7%)
  local copies, waits for them, and re-layouts  6.99 us (6%)
    all_to_all x1, waiting for transfers between devices, body(): lax.all_to_all(partial_value, 'neuron', split_axis=0, concat_axis=0, tile...  36.1 us
    all_to_all x1, waiting for transfers between devices, body(): lax.all_to_all(outgoing, 'neuron', split_axis=0, concat_axis=0, tiled=True)  36 us
    dot_general x1, matrix products, body(): jnp.dot(hidden, w_out, preferred_element_type=jnp.float32)  8.4 us
    all_to_all x1, starting transfers between devices, body(): lax.all_to_all(outgoing_flags, 'neuron', split_axis=0, concat_axis=0, til...  6.55 us
    all_to_all x1, starting transfers between devices, body(): lax.all_to_all(outgoing, 'neuron', split_axis=0, concat_axis=0, tiled=True)  6.15 us
    all_to_all x1, starting transfers between devices, body(): lax.all_to_all(partial_value, 'neuron', split_axis=0, concat_axis=0, tile...  5.04 us
  transfers between devices with their start and end apart: 3, of which 2 were waited for; matrix products, arithmetic and copies ran while one was open for 8% of the time, Pallas kernels for 0%

commit v1 on v0

v1 whole, which is shorter than its diff:
```python
import functools

import jax
import jax.numpy as jnp
from jax import lax
from jax.experimental import pallas as pl
from jax.experimental.pallas import tpu as pltpu
from jax.sharding import PartitionSpec as P

BLK = 128
LANES = 128
SUB = 8
VMEM_LIMIT = 56 * 1024 * 1024

epsilon = 1e-05


def route_matrix(active_ref, row_count, col_count, per_device, nodes, transposed):
    requests, active = active_ref.shape
    shape = (col_count, row_count) if transposed else (row_count, col_count)
    slot = lax.broadcasted_iota(jnp.int32, shape, 1 if transposed else 0)
    item = lax.broadcasted_iota(jnp.int32, shape, 0 if transposed else 1)
    per_half = requests * nodes
    device, inner = slot // SUB, slot % SUB
    half, request, node = item // per_half, (item % per_half) // nodes, item % nodes
    aligned = inner == half * nodes + node
    touched = jnp.zeros(shape, jnp.bool_)
    for r in range(requests):
        for a in range(active):
            touched = touched | ((request == r) & (device == active_ref[r, a] // per_device))
    return jnp.where(touched & aligned, 1.0, 0.0)


def send_kernel(active_ref, tokens_ref, gain_ref, bias_ref, out_ref, *, per_device, nodes):
    rows, features = tokens_ref.shape
    half = features // 2
    slots = out_ref.shape[0]
    requests, active = active_ref.shape
    total = jnp.zeros((rows, LANES), jnp.float32)
    for j in range(0, features, LANES):
        total += tokens_ref[:, j : j + LANES].astype(jnp.float32)
    mean = jnp.sum(total, axis=1, keepdims=True) / features
    total = jnp.zeros((rows, LANES), jnp.float32)
    for j in range(0, features, LANES):
        centred = tokens_ref[:, j : j + LANES].astype(jnp.float32) - mean
        total += centred * centred
    scale = lax.rsqrt(jnp.sum(total, axis=1, keepdims=True) / features + epsilon)
    route = route_matrix(active_ref, slots, 2 * rows, per_device, nodes, False).astype(jnp.bfloat16)

    def normed(start, width):
        centred = tokens_ref[:, pl.ds(start, width)].astype(jnp.float32) - mean
        gain = gain_ref[:, pl.ds(start, width)].astype(jnp.float32)
        bias = bias_ref[:, pl.ds(start, width)].astype(jnp.float32)
        return (centred * scale * gain + bias).astype(jnp.bfloat16)

    width = 512
    for j in range(0, half, width):
        both = jnp.concatenate([normed(j, width), normed(half + j, width)], axis=0)
        out_ref[:, j : j + width] = jnp.dot(route, both, preferred_element_type=jnp.float32).astype(jnp.bfloat16)
    device = lax.broadcasted_iota(jnp.int32, (slots, LANES), 0) // SUB
    lane = lax.broadcasted_iota(jnp.int32, (slots, LANES), 1)
    flags = jnp.zeros((slots, LANES), jnp.bool_)
    for r in range(requests):
        for a in range(active):
            block = active_ref[r, a]
            flags = flags | ((device == block // per_device) & (lane == block % per_device))
    out_ref[:, half:] = jnp.where(flags, 1.0, 0.0).astype(jnp.bfloat16)


def neuron_kernel(x_ref, w_in_hbm, b_in_ref, w_out_hbm, out_ref, w_in, w_out, in_sem, out_sem, *, nodes, parts):
    slots = x_ref.shape[0]
    features, units = w_in.shape
    half = features // 2
    depth, width = half // parts, half // parts
    in_copies, out_copies = [], []
    for k in range(2 * parts):
        span = pl.ds(k * depth, depth)
        in_copies.append(pltpu.make_async_copy(w_in_hbm.at[span, :], w_in.at[span, :], in_sem.at[k]))
        in_copies[-1].start()
    for k in range(2 * parts):
        span = pl.ds(k * width, width)
        out_copies.append(pltpu.make_async_copy(w_out_hbm.at[:, span], w_out.at[:, span], out_sem.at[k]))
    for k in range(parts):
        out_copies[k].start()
        out_copies[parts + k].start()
    sums = []
    for h in range(2):
        total = jnp.zeros((slots, units), jnp.float32)
        for k in range(parts):
            in_copies[h * parts + k].wait()
            at = h * half + k * depth
            total += jnp.dot(
                x_ref[:, k * depth : (k + 1) * depth],
                w_in[at : at + depth, :],
                preferred_element_type=jnp.float32,
            )
        sums.append(total)
    first, second = sums
    upper = lax.broadcasted_iota(jnp.int32, (slots, 1), 0) % SUB < nodes
    preact = jnp.where(
        upper,
        first + pltpu.roll(second, slots - nodes, 0),
        second + pltpu.roll(first, nodes, 0),
    ) + b_in_ref[...].astype(jnp.float32)
    hidden = []
    for b in range(units // BLK):
        flag = x_ref[:, half : half + LANES].astype(jnp.float32)[:, b : b + 1]
        hidden.append(jnp.maximum(preact[:, b * BLK : (b + 1) * BLK], 0.0) * flag)
    hidden = jnp.concatenate(hidden, axis=1).astype(jnp.bfloat16)
    for k in range(parts):
        out_copies[k].wait()
        out_copies[parts + k].wait()
        at = k * width
        lo = jnp.dot(hidden, w_out[:, at : at + width], preferred_element_type=jnp.float32)
        hi = jnp.dot(hidden, w_out[:, half + at : half + at + width], preferred_element_type=jnp.float32)
        out_ref[:, at : at + width] = jnp.where(upper, lo, hi).astype(jnp.bfloat16)


def finish_kernel(active_ref, returned_ref, tokens_ref, b_out_ref, out_ref, *, per_device, nodes):
    rows, features = tokens_ref.shape
    half = features // 2
    slots = returned_ref.shape[0]
    route = route_matrix(active_ref, slots, 2 * rows, per_device, nodes, True).astype(jnp.bfloat16)
    width = 512
    for j in range(0, half, width):
        both = jnp.dot(route, returned_ref[:, j : j + width], preferred_element_type=jnp.float32)
        for h in range(2):
            at = h * half + j
            mixed = (
                tokens_ref[:, at : at + width].astype(jnp.float32)
                + both[h * rows : (h + 1) * rows]
                + b_out_ref[:, at : at + width].astype(jnp.float32)
            )
            out_ref[:, at : at + width] = mixed.astype(jnp.bfloat16)


def body(tokens, active, ln_gain, ln_bias, w_in, b_in, w_out, b_out):
    rows, features = tokens.shape
    requests = active.shape[0]
    nodes = rows // requests
    units = w_in.shape[1]
    half = features // 2
    device_count = lax.axis_size("neuron")
    per_device = units // BLK
    slots = device_count * SUB
    params = pltpu.CompilerParams(vmem_limit_bytes=VMEM_LIMIT)
    smem = pl.BlockSpec(memory_space=pltpu.SMEM)
    vmem = pl.BlockSpec(memory_space=pltpu.VMEM)
    outgoing = pl.pallas_call(
        functools.partial(send_kernel, per_device=per_device, nodes=nodes),
        out_shape=jax.ShapeDtypeStruct((slots, half + LANES), jnp.bfloat16),
        in_specs=[smem, vmem, vmem, vmem],
        out_specs=vmem,
        compiler_params=params,
    )(active, tokens, ln_gain[None], ln_bias[None])
    arrived = lax.all_to_all(
        outgoing.reshape(device_count, SUB, half + LANES), "neuron", split_axis=0, concat_axis=0, tiled=True
    ).reshape(slots, half + LANES)
    parts = 4
    block = min(slots, 16 * SUB)
    hbm = pl.BlockSpec(memory_space=pl.ANY)
    partial_value = pl.pallas_call(
        functools.partial(neuron_kernel, nodes=nodes, parts=parts),
        out_shape=jax.ShapeDtypeStruct((slots, half), jnp.bfloat16),
        grid=(slots // block,),
        in_specs=[
            pl.BlockSpec((block, half + LANES), lambda i: (i, 0)),
            hbm,
            pl.BlockSpec((1, units), lambda i: (0, 0)),
            hbm,
        ],
        out_specs=pl.BlockSpec((block, half), lambda i: (i, 0)),
        scratch_shapes=[
            pltpu.VMEM((features, units), jnp.bfloat16),
            pltpu.VMEM((units, features), jnp.bfloat16),
            pltpu.SemaphoreType.DMA((2 * parts,)),
            pltpu.SemaphoreType.DMA((2 * parts,)),
        ],
        compiler_params=params,
    )(arrived, w_in, b_in[None], w_out)
    returned = lax.all_to_all(
        partial_value.reshape(device_count, SUB, half), "neuron", split_axis=0, concat_axis=0, tiled=True
    ).reshape(slots, half)
    return pl.pallas_call(
        functools.partial(finish_kernel, per_device=per_device, nodes=nodes),
        out_shape=jax.ShapeDtypeStruct((rows, features), jnp.bfloat16),
        in_specs=[smem, vmem, vmem, vmem],
        out_specs=vmem,
        compiler_params=params,
    )(active, returned, tokens, b_out[None])


def solution(mesh):
    placed = (
        P(("groups", "neuron"), None),
        P(("groups", "neuron"), None),
        P(),
        P(),
        P(None, "neuron"),
        P("neuron"),
        P("neuron", None),
        P(),
    )
    return jax.shard_map(
        body, mesh=mesh, in_specs=placed, out_specs=P(("groups", "neuron"), None), check_vma=False
    )
```

time: 116 us -> 105 us (0.905)
  Pallas kernels: 0 us -> 15.2 us
  matrix products: 10.2 us -> 0 us
  other arithmetic: 8.23 us -> 0 us
  starting transfers between devices: 17.7 us -> 11.6 us
    pallas_call x0 -> x3, Pallas kernels: none -> 15.2 us  [the longest x1 8.99 us: body(): pl.pallas_call(functools.partial(neuron_kernel, nodes=nodes, parts=parts)...]
    dot_general x2 -> x0, matrix products: 10.2 us -> none  [the longest x1 8.4 us: body(): jnp.dot(hidden, w_out, preferred_element_type=jnp.float32)]
    all_to_all x3 -> x2, starting transfers between devices: 17.7 us -> 11.6 us  [the longest x1 6.69 us: body(): lax.all_to_all(outgoing.reshape(device_count, SUB, half + LANES), 'neuron...]
    convert_element_type x8 -> x0, other arithmetic: 3.66 us -> none  [the longest x1 1.21 us: layer_norm(): (scaled * ln_gain.astype(jnp.float32) + ln_bias.astype(jnp.float32)).asty...]
    broadcast_in_dim x3 -> x4, local copies, waits for them, and re-layouts: 0.9 us -> 3.97 us  [the longest x1 1.38 us: body(): ln_gain[None]]
    reduce_sum x3 -> x0, other arithmetic: 2.58 us -> none  [the longest x1 1.28 us: layer_norm(): row_var = jnp.mean(centred * centred, axis=1, keepdims=True)]
    reshape x4 -> x0, local copies, waits for them, and re-layouts: 2.31 us -> none  [the longest x1 1.5 us: body(): partial_value.reshape(device_count, item_count, feature_count)]
    select_n x2 -> x0, other arithmetic: 1.92 us -> none  [body(): outgoing = jnp.take(by_request, chosen, axis=0)]
  transfers between devices with their start and end apart: 3 -> 2, of which waited for: 2 -> 2; matrix products, arithmetic and copies ran while one was open for 8% -> 1% of each run, Pallas kernels for 0% -> 0%
where the time goes in v1:
time: 105 us
  waiting for transfers between devices  71.8 us (68%)
  Pallas kernels  15.2 us (14%)
  starting transfers between devices  11.6 us (11%)
  local copies, waits for them, and re-layouts  6.28 us (6%)
    all_to_all x1, waiting for transfers between devices, body(): lax.all_to_all(outgoing.reshape(device_count, SUB, half + LANES), 'neuron...  36.3 us
    all_to_all x1, waiting for transfers between devices, body(): lax.all_to_all(partial_value.reshape(device_count, SUB, half), 'neuron',...  35.5 us
    pallas_call x1, Pallas kernels, body(): pl.pallas_call(functools.partial(neuron_kernel, nodes=nodes, parts=parts)...  8.99 us
    all_to_all x1, starting transfers between devices, body(): lax.all_to_all(outgoing.reshape(device_count, SUB, half + LANES), 'neuron...  6.69 us
    all_to_all x1, starting transfers between devices, body(): lax.all_to_all(partial_value.reshape(device_count, SUB, half), 'neuron',...  4.93 us
    pallas_call x1, Pallas kernels, body(): pl.pallas_call(functools.partial(send_kernel, per_device=per_device, node...  3.51 us
    pallas_call x1, Pallas kernels, body(): pl.pallas_call(functools.partial(finish_kernel, per_device=per_device, no...  2.69 us
    unnamed x8, local copies, waits for them, and re-layouts  2.31 us
  transfers between devices with their start and end apart: 2, of which 2 were waited for; matrix products, arithmetic and copies ran while one was open for 1% of the time, Pallas kernels for 0%

profile of v1, /device:TPU:15, one launch (start us, length us, event | category | flops | bytes accessed | tf_op | source)
XLA Modules:
  0.0 105.0 jit_solution(154526206594106048)
XLA Ops:
  0.0 1.4 %broadcast_in_dim.12.gain_ref = bf16[1,12288]{1,0:T(2,128)(2,1)} reshape(bf16[12288]{0:T(1024)(128)(2,1)} %param.10) | data formatting | bytes 49152 | tf_op jit(solution)/shard_map/broadcast_in_dim | solution.py:155
  1.4 1.4 %broadcast_in_dim.13.bias_ref = bf16[1,12288]{1,0:T(2,128)(2,1)} reshape(bf16[12288]{0:T(1024)(128)(2,1)} %param.11) | data formatting | bytes 49152 | tf_op jit(solution)/shard_map/broadcast_in_dim | solution.py:155
  2.8 3.5 %shard_map.82 = bf16[128,6272]{1,0:T(8,128)(2,1)} custom-call(s32[4,3]{1,0:T(4,128)} %active_ref.3, bf16[16,12288]{1,0:T(8,128)(2,1)} %tokens_ref.3, bf16[1,12288]{1,0:T(2,128)(2,1)} %broadcast_in_dim.12.gain_ref, bf16[1,12288]{1,0:T(2,128)(2,1)} %broadcast_in_dim.13.bias_ref), custom_call_target="tpu_custom_call" | custom-call | tf_op jit(solution)/shard_map/pallas_call | solution.py:149
  6.3 0.0 copy-start.3
  6.3 6.7 %all-to-all-start = ((bf16[16,8,6272]{2,1,0:T(8,128)(2,1)}), bf16[16,8,6272]{2,1,0:T(8,128)(2,1)S(1)}, u32[]{:S(2)}, u32[]{:S(2)}) async-start(bf16[16,8,6272]{2,1,0:T(8,128)(2,1)} %bitcast.4), calls=%async_computation | async-start | bytes 3211264 | tf_op jit(solution)/shard_map/all_to_all | solution.py:156
  13.0 0.0 copy-done.3
  13.0 0.6 broadcast_in_dim.14.b_in_ref
  13.5 36.3 %all-to-all-done = bf16[16,8,6272]{2,1,0:T(8,128)(2,1)S(1)} async-done(((bf16[16,8,6272]{2,1,0:T(8,128)(2,1)}), bf16[16,8,6272]{2,1,0:T(8,128)(2,1)S(1)}, u32[]{:S(2)}, u32[]{:S(2)}) %all-to-all-start) | async-done | bytes 1605664 | tf_op jit(solution)/shard_map/all_to_all | solution.py:156
  49.9 0.0 copy-start
  49.9 1.2 %copy-done = bf16[16,8,6272]{2,1,0:T(8,128)(2,1)} copy-done((bf16[16,8,6272]{2,1,0:T(8,128)(2,1)}, bf16[16,8,6272]{2,1,0:T(8,128)(2,1)S(1)}, u32[]{:S(2)}) %copy-start) | copy-done | bytes 1605656
  51.0 9.0 %shard_map.83 = bf16[128,6144]{1,0:T(8,128)(2,1)} custom-call(bf16[128,6272]{1,0:T(8,128)(2,1)} %bitcast.5, bf16[12288,256]{1,0:T(8,128)(2,1)} %w_in_hbm.1, bf16[1,256]{1,0:T(2,128)(2,1)} %broadcast_in_dim.14.b_in_ref, bf16[256,12288]{1,0:T(8,128)(2,1)} %w_out_hbm.1), custom_call_target="tpu_custom_call" | custom-call | tf_op jit(solution)/shard_map/pallas_call | solution.py:162
  60.0 0.0 copy-start.2
  60.0 4.9 %all-to-all-start.1 = ((bf16[16,8,6144]{2,1,0:T(8,128)(2,1)}), bf16[16,8,6144]{2,1,0:T(8,128)(2,1)S(1)}, u32[]{:S(2)}, u32[]{:S(2)}) async-start(bf16[16,8,6144]{2,1,0:T(8,128)(2,1)} %bitcast.7), calls=%async_computation.1 | async-start | bytes 3145728 | tf_op jit(solution)/shard_map/all_to_all | solution.py:181
  65.0 0.0 copy-done.2
  65.0 0.6 broadcast_in_dim.15.b_out_ref
  65.6 35.5 %all-to-all-done.1 = bf16[16,8,6144]{2,1,0:T(8,128)(2,1)S(1)} async-done(((bf16[16,8,6144]{2,1,0:T(8,128)(2,1)}), bf16[16,8,6144]{2,1,0:T(8,128)(2,1)S(1)}, u32[]{:S(2)}, u32[]{:S(2)}) %all-to-all-start.1) | async-done | bytes 1572896 | tf_op jit(solution)/shard_map/all_to_all | solution.py:181
  101.1 0.0 copy-start.1
  101.1 1.1 %copy-done.1 = bf16[16,8,6144]{2,1,0:T(8,128)(2,1)} copy-done((bf16[16,8,6144]{2,1,0:T(8,128)(2,1)}, bf16[16,8,6144]{2,1,0:T(8,128)(2,1)S(1)}, u32[]{:S(2)}) %copy-start.1) | copy-done | bytes 1572888
  102.3 2.7 %shard_map.84 = bf16[16,12288]{1,0:T(8,128)(2,1)} custom-call(s32[4,3]{1,0:T(4,128)} %active_ref.3, bf16[128,6144]{1,0:T(8,128)(2,1)} %bitcast.6, bf16[16,12288]{1,0:T(8,128)(2,1)} %tokens_ref.3, bf16[1,12288]{1,0:T(2,128)(2,1)} %broadcast_in_dim.15.b_out_ref), custom_call_target="tpu_custom_call" | custom-call | tf_op jit(solution)/shard_map/pallas_call | solution.py:184
Async XLA Ops:
  6.3 6.7 %copy-start.3 = (bf16[256]{0:T(256)(128)(2,1)S(1)}, bf16[256]{0:T(256)(128)(2,1)}, u32[]{:S(2)}) copy-start(bf16[256]{0:T(256)(128)(2,1)} %param.13) | copy-start | bytes 1540
  6.3 43.6 %all-to-all-start = ((bf16[16,8,6272]{2,1,0:T(8,128)(2,1)}), bf16[16,8,6272]{2,1,0:T(8,128)(2,1)S(1)}, u32[]{:S(2)}, u32[]{:S(2)}) async-start(bf16[16,8,6272]{2,1,0:T(8,128)(2,1)} %bitcast.4), calls=%async_computation | async-start | bytes 3211264 | tf_op jit(solution)/shard_map/all_to_all | solution.py:156
  49.9 1.2 %copy-start = (bf16[16,8,6272]{2,1,0:T(8,128)(2,1)}, bf16[16,8,6272]{2,1,0:T(8,128)(2,1)S(1)}, u32[]{:S(2)}) copy-start(bf16[16,8,6272]{2,1,0:T(8,128)(2,1)S(1)} %all-to-all-done) | copy-start | bytes 4816900
  60.0 4.9 %copy-start.2 = (bf16[12288]{0:T(1024)(128)(2,1)S(1)}, bf16[12288]{0:T(1024)(128)(2,1)}, u32[]{:S(2)}) copy-start(bf16[12288]{0:T(1024)(128)(2,1)} %param.15) | copy-start | bytes 73732
  60.0 41.1 %all-to-all-start.1 = ((bf16[16,8,6144]{2,1,0:T(8,128)(2,1)}), bf16[16,8,6144]{2,1,0:T(8,128)(2,1)S(1)}, u32[]{:S(2)}, u32[]{:S(2)}) async-start(bf16[16,8,6144]{2,1,0:T(8,128)(2,1)} %bitcast.7), calls=%async_computation.1 | async-start | bytes 3145728 | tf_op jit(solution)/shard_map/all_to_all | solution.py:181
  101.1 1.1 %copy-start.1 = (bf16[16,8,6144]{2,1,0:T(8,128)(2,1)}, bf16[16,8,6144]{2,1,0:T(8,128)(2,1)S(1)}, u32[]{:S(2)}) copy-start(bf16[16,8,6144]{2,1,0:T(8,128)(2,1)S(1)} %all-to-all-done.1) | copy-start | bytes 4718596

commit v2 on v0

v2 whole, which is shorter than its diff:
```python
import functools

import jax
import jax.numpy as jnp
from jax import lax
from jax.experimental import pallas as pl
from jax.experimental.pallas import tpu as pltpu
from jax.sharding import PartitionSpec as P

BLK = 128
LANES = 128
SUB = 8
WIDTH = 512
MIB = 1024 * 1024
SELECT_COST = 10_000_000_000

epsilon = 1e-05


def iota(shape, axis):
    return lax.broadcasted_iota(jnp.int32, shape, axis)


def touches(ids, device, per_device, active):
    owner = (ids.astype(jnp.int32) + (per_device - 1)) // per_device - 1
    touched = jnp.zeros(device.shape, jnp.bool_)
    for a in range(active):
        touched = touched | (owner[:, a : a + 1] == device)
    return touched


def spread_matrix(ids, first_device, device_count, per_device, active):
    shape = (ids.shape[0], device_count * SUB)
    wanted = iota(shape, 1) % SUB == iota(shape, 0) % SUB
    touched = touches(ids, first_device + iota(shape, 1) // SUB, per_device, active)
    return jnp.where(touched & wanted, 1.0, 0.0)


def near_matrix(ids, chips, per_device, active):
    shape = (ids.shape[0], chips * SUB)
    wanted = iota(shape, 1) % SUB == iota(shape, 0) % SUB
    me = lax.axis_index("neuron")
    device = 2 * (me // 2 ^ iota(shape, 1) // SUB) + me % 2
    return jnp.where(touches(ids, device, per_device, active) & wanted, 1.0, 0.0)


def half_start(half_count):
    return lax.axis_index("neuron") // half_count * half_count


def norm_kernel(active_ref, tokens_ref, gain_ref, bias_ref, out_ref, *, nodes):
    rows, features = tokens_ref.shape
    half = features // 2
    packed = 2 * rows
    requests, active = active_ref.shape
    total = jnp.zeros((rows, LANES), jnp.float32)
    for j in range(0, features, LANES):
        total += tokens_ref[:, j : j + LANES].astype(jnp.float32)
    mean = jnp.sum(total, axis=1, keepdims=True) / features
    total = jnp.zeros((rows, LANES), jnp.float32)
    for j in range(0, features, LANES):
        centred = tokens_ref[:, j : j + LANES].astype(jnp.float32) - mean
        total += centred * centred
    scale = lax.rsqrt(jnp.sum(total, axis=1, keepdims=True) / features + epsilon)
    shape = (packed, packed)
    slot, item = iota(shape, 0), iota(shape, 1)
    source = (slot % SUB // nodes) * rows + slot // SUB * nodes + slot % nodes
    pack = jnp.where(item == source, 1.0, 0.0).astype(jnp.bfloat16)

    def normed(start):
        centred = tokens_ref[:, start : start + WIDTH].astype(jnp.float32) - mean
        gain = gain_ref[start : start + WIDTH].astype(jnp.float32).reshape(1, WIDTH)
        bias = bias_ref[start : start + WIDTH].astype(jnp.float32).reshape(1, WIDTH)
        return (centred * scale * gain + bias).astype(jnp.bfloat16)

    for j in range(0, half, WIDTH):
        both = jnp.concatenate([normed(j), normed(half + j)], axis=0)
        out_ref[:, j : j + WIDTH] = jnp.dot(pack, both, preferred_element_type=jnp.float32).astype(jnp.bfloat16)
    request, lane = iota((packed, LANES), 0) // SUB, iota((packed, LANES), 1)
    ids = jnp.zeros((packed, LANES), jnp.int32)
    for r in range(requests):
        for a in range(active):
            ids = jnp.where((request == r) & (lane == a), active_ref[r, a] + 1, ids)
    out_ref[:, half:] = ids.astype(jnp.float32).astype(jnp.bfloat16)


def select_kernel(packed_ref, *refs, half_count, per_device, active):
    out_ref = refs[-1]
    total = packed_ref.shape[1]
    half = total - LANES
    ids = packed_ref[:, half:].astype(jnp.float32)
    spread = spread_matrix(ids, half_start(half_count), half_count, per_device, active)
    chosen = spread.T.astype(jnp.bfloat16)
    for j in list(range(0, half, WIDTH)) + [half]:
        span = slice(j, min(j + WIDTH, total) if j < half else total)
        out_ref[:, span] = jnp.dot(chosen, packed_ref[:, span], preferred_element_type=jnp.float32).astype(jnp.bfloat16)


def select_near_kernel(own_ref, mate_ref, *out_refs, per_device, active):
    total = own_ref.shape[1]
    half = total - LANES
    chips = len(out_refs)
    for s, packed_ref in enumerate((own_ref, mate_ref)):
        ids = packed_ref[:, half:].astype(jnp.float32)
        chosen = near_matrix(ids, chips, per_device, active).T.astype(jnp.bfloat16)
        for j in list(range(0, half, WIDTH)) + [half]:
            span = slice(j, min(j + WIDTH, total) if j < half else total)
            rows = jnp.dot(chosen, packed_ref[:, span], preferred_element_type=jnp.float32)
            for k, out_ref in enumerate(out_refs):
                out_ref[s * SUB : (s + 1) * SUB, span] = rows[k * SUB : (k + 1) * SUB].astype(jnp.bfloat16)


def neuron_kernel(*refs, nodes, chips):
    near_refs, refs = refs[:chips], refs[chips:]
    far_ref, w_in_ref, b_in_ref, w_out_ref = refs[:4]
    near_out_refs, far_out_ref, x_ref = refs[4:-2], refs[-2], refs[-1]
    slots = x_ref.shape[0]
    features, units = w_in_ref.shape
    half = features // 2
    per_device = units // BLK
    depth = half // 4
    for k, near_ref in enumerate(near_refs):
        x_ref[2 * SUB * k : 2 * SUB * (k + 1), :] = near_ref[...]
    near_rows = 2 * SUB * chips
    x_ref[near_rows:, :] = far_ref[...]
    sums = []
    for h in range(2):
        total = jnp.zeros((slots, units), jnp.float32)
        for at in range(0, half, depth):
            total += jnp.dot(
                x_ref[:, at : at + depth],
                w_in_ref[h * half + at : h * half + at + depth, :],
                preferred_element_type=jnp.float32,
            )
        sums.append(total)
    first, second = sums
    upper = iota((slots, 1), 0) % SUB < nodes
    preact = jnp.where(
        upper,
        first + pltpu.roll(second, slots - nodes, 0),
        second + pltpu.roll(first, nodes, 0),
    ) + b_in_ref[...].astype(jnp.float32).reshape(1, units)
    ids = x_ref[:, half : half + LANES].astype(jnp.float32).astype(jnp.int32)
    own = lax.axis_index("neuron") * per_device + 1
    hidden = []
    for b in range(per_device):
        flag = jnp.max(jnp.where(ids == own + b, 1.0, 0.0), axis=1, keepdims=True)
        hidden.append(jnp.maximum(preact[:, b * BLK : (b + 1) * BLK], 0.0) * flag)
    hidden = jnp.concatenate(hidden, axis=1).astype(jnp.bfloat16)
    for at in range(0, half, depth):
        lo = jnp.dot(hidden, w_out_ref[:, at : at + depth], preferred_element_type=jnp.float32)
        hi = jnp.dot(hidden, w_out_ref[:, half + at : half + at + depth], preferred_element_type=jnp.float32)
        both = jnp.where(upper, lo, hi).astype(jnp.bfloat16)
        for k, near_out_ref in enumerate(near_out_refs):
            near_out_ref[:, at : at + depth] = both[2 * SUB * k : 2 * SUB * (k + 1)]
        far_out_ref[:, at : at + depth] = both[near_rows:]


def gather_kernel(packed_ref, returned_ref, *refs, half_count, per_device, active):
    half = returned_ref.shape[1]
    count = len(refs) // 2
    out_ref = refs[count]
    for part_ref, copy_ref in zip(refs[:count], refs[count + 1 :], strict=True):
        copy_ref[...] = part_ref[...]
    ids = packed_ref[:, half:].astype(jnp.float32)
    spread = spread_matrix(ids, half_start(half_count), half_count, per_device, active).astype(jnp.bfloat16)
    for j in range(0, half, WIDTH):
        part = jnp.dot(spread, returned_ref[:, j : j + WIDTH], preferred_element_type=jnp.float32)
        out_ref[:, j : j + WIDTH] = part.astype(jnp.bfloat16)


def gather_near_kernel(own_ref, mate_ref, *refs, per_device, active):
    back_refs, out_refs = refs[:-2], refs[-2:]
    half = back_refs[0].shape[1]
    chips = len(back_refs)
    for s, packed_ref in enumerate((own_ref, mate_ref)):
        spread = near_matrix(packed_ref[:, half:].astype(jnp.float32), chips, per_device, active).astype(jnp.bfloat16)
        for j in range(0, half, WIDTH):
            back = jnp.concatenate([ref[s * SUB : (s + 1) * SUB, j : j + WIDTH] for ref in back_refs], axis=0)
            part = jnp.dot(spread, back, preferred_element_type=jnp.float32)
            out_refs[s][:, j : j + WIDTH] = part.astype(jnp.bfloat16)


def finish_kernel(near_ref, mate_ref, far_ref, tokens_ref, b_out_ref, out_ref, *, nodes):
    rows, features = tokens_ref.shape
    half = features // 2
    shape = (2 * rows, 2 * rows)
    item, slot = iota(shape, 0), iota(shape, 1)
    source = item % rows // nodes * SUB + item // rows * nodes + item % nodes
    unpack = jnp.where(slot == source, 1.0, 0.0).astype(jnp.bfloat16)
    for j in range(0, half, WIDTH):
        both = jnp.zeros((2 * rows, WIDTH), jnp.float32)
        for ref in (near_ref, mate_ref, far_ref):
            both += jnp.dot(unpack, ref[:, j : j + WIDTH], preferred_element_type=jnp.float32)
        for h in range(2):
            at = h * half + j
            mixed = (
                tokens_ref[:, at : at + WIDTH].astype(jnp.float32)
                + both[h * rows : (h + 1) * rows]
                + b_out_ref[at : at + WIDTH].astype(jnp.float32).reshape(1, WIDTH)
            )
            out_ref[:, at : at + WIDTH] = mixed.astype(jnp.bfloat16)


def body(tokens, active, ln_gain, ln_bias, w_in, b_in, w_out, b_out):
    rows, features = tokens.shape
    requests, active_count = active.shape
    nodes = rows // requests
    units = w_in.shape[1]
    half = features // 2
    device_count = lax.axis_size("neuron")
    half_count = device_count // 2
    per_device = units // BLK
    packed = requests * SUB
    slots = half_count * SUB
    smem = pl.BlockSpec(memory_space=pltpu.SMEM)
    vmem = pl.BlockSpec(memory_space=pltpu.VMEM)
    hbm = pl.BlockSpec(memory_space=pl.ANY)
    chips = half_count // 2
    halves = [list(range(half_count)), list(range(half_count, device_count))]
    routing = dict(per_device=per_device, active=active_count)

    def call(kernel, shapes, in_specs, *operands, scratch=(), cost=0, limit=0):
        size = 2 * sum(rows * columns for rows, columns in shapes) + sum(x.size * 2 for x in operands)
        size += sum(2 * rows * columns for rows, columns in scratch)
        return pl.pallas_call(
            kernel,
            out_shape=[jax.ShapeDtypeStruct(shape, jnp.bfloat16) for shape in shapes],
            in_specs=in_specs,
            out_specs=[vmem] * len(shapes),
            scratch_shapes=[pltpu.VMEM(shape, jnp.bfloat16) for shape in scratch],
            compiler_params=pltpu.CompilerParams(vmem_limit_bytes=max(size + 8 * MIB, limit)),
            cost_estimate=pl.CostEstimate(flops=cost, bytes_accessed=size, transcendentals=0),
        )(*operands)

    def swap(x, partner):
        return lax.ppermute(x, "neuron", [(i, partner(i)) for i in range(device_count)])

    def across(x):
        return swap(x, lambda i: (i + half_count) % device_count)

    def mate_of(x):
        return swap(x, lambda i: i ^ 1)

    def to_chips(xs):
        return [xs[0]] + [swap(x, lambda i, k=k: i ^ 2 * k) for k, x in enumerate(xs) if k]

    def exchange(x):
        width = x.shape[1]
        return lax.all_to_all(
            x.reshape(half_count, SUB, width), "neuron", 0, 0, axis_index_groups=halves, tiled=True
        ).reshape(slots, width)

    [own] = call(
        functools.partial(norm_kernel, nodes=nodes),
        [(packed, half + LANES)],
        [smem, vmem, vmem, vmem],
        active, tokens, ln_gain, ln_bias,
        limit=56 * MIB,
    )
    other = across(own)
    mate = mate_of(own)
    near_slots = call(
        functools.partial(select_near_kernel, **routing),
        [(2 * SUB, half + LANES)] * chips,
        [vmem] * 2,
        own, mate,
    )
    near_rows = to_chips(near_slots)
    [far_slots] = call(
        functools.partial(select_kernel, half_count=half_count, **routing),
        [(slots, half + LANES)],
        [vmem] + [hbm] * (chips - 1),
        other, *near_rows[1:],
        cost=SELECT_COST,
    )
    far_rows = exchange(far_slots)
    *near_parts, far_part = call(
        functools.partial(neuron_kernel, nodes=nodes, chips=chips),
        [(2 * SUB, half)] * chips + [(slots, half)],
        [vmem] * (chips + 4),
        *near_rows, far_rows, w_in, b_in, w_out,
        scratch=[(2 * slots, half + LANES)],
    )
    far_back = exchange(far_part)
    gathered, *near_sent = call(
        functools.partial(gather_kernel, half_count=half_count, **routing),
        [(packed, half)] + [(2 * SUB, half)] * (chips - 1),
        [vmem] * (1 + chips),
        other, far_back, *near_parts[1:],
    )
    far_sum = across(gathered)
    near_own, near_mate = call(
        functools.partial(gather_near_kernel, **routing),
        [(packed, half)] * 2,
        [vmem] * (2 + chips),
        own, mate, *to_chips([near_parts[0], *near_sent]),
    )
    [mixed] = call(
        functools.partial(finish_kernel, nodes=nodes),
        [(rows, features)],
        [vmem] * 5,
        near_own, mate_of(near_mate), far_sum, tokens, b_out,
    )
    return mixed


def solution(mesh):
    placed = (
        P(("groups", "neuron"), None),
        P(("groups", "neuron"), None),
        P(),
        P(),
        P(None, "neuron"),
        P("neuron"),
        P("neuron", None),
        P(),
    )
    return jax.shard_map(
        body, mesh=mesh, in_specs=placed, out_specs=P(("groups", "neuron"), None), check_vma=False
    )
```

time: 116 us -> 86.3 us (0.74)
  the two profiles are of different devices: /device:TPU:15 before, /device:TPU:0 now
where the time goes in v2:
time: 86.3 us; the launch traced here: 86 us
  waiting for transfers between devices  32.7 us (38%)
  blocking collectives  29.5 us (34%)
  starting transfers between devices  15.2 us (18%)
  Pallas kernels  7.5 us (9%)
  local copies, waits for them, and re-layouts  1.07 us (1%)
    ppermute x10, waiting for transfers between devices, swap(): lax.ppermute(x, 'neuron', [(i, partner(i)) for i in range(device_count)])  32.7 us
    all_to_all x2, blocking collectives, exchange(): lax.all_to_all(x.reshape(half_count, SUB, width), 'neuron', 0, 0, axis_in...  29.5 us
    ppermute x10, starting transfers between devices, swap(): lax.ppermute(x, 'neuron', [(i, partner(i)) for i in range(device_count)])  15.2 us
    pallas_call x7, Pallas kernels, call(): pl.pallas_call(kernel, out_shape=[jax.ShapeDtypeStruct(shape, jnp.bfloat1...  7.5 us
  transfers between devices with their start and end apart: 10, of which 5 were waited for; matrix products, arithmetic and copies ran while one was open for 0% of the time, Pallas kernels for 1%

profile of v2, /device:TPU:0, one launch (start us, length us, event | category | flops | bytes accessed | tf_op | source)
XLA Modules:
  0.0 86.0 jit_solution(4641362382562213454)
XLA Ops:
  0.0 2.5 %shard_map.82.own_ref = bf16[32,6272]{1,0:T(8,128)(2,1)} custom-call(s32[4,3]{1,0:T(4,128)} %active_ref.1, bf16[16,12288]{1,0:T(8,128)(2,1)} %tokens_ref.3, bf16[12288]{0:T(1024)(128)(2,1)} %gain_ref.1, bf16[12288]{0:T(1024)(128)(2,1)} %bias_ref.1), custom_call_target="tpu_custom_call" | custom-call | bytes 843800 | tf_op jit(solution)/shard_map/pallas_call | solution.py:226
  2.5 0.5 collective-permute-start
  2.9 3.6 %collective-permute-start.4 = (bf16[32,6272]{1,0:T(8,128)(2,1)}, bf16[32,6272]{1,0:T(8,128)(2,1)S(1)}, u32[]{:S(2)}, u32[]{:S(2)}) collective-permute-start(bf16[32,6272]{1,0:T(8,128)(2,1)} %shard_map.82.own_ref), channel_id=1, source_target_pairs={{0,8},{1,9},{2,10},{3,11},{4,12},{5,13},{6,14},{7,15},{8,0},{9,1},... | collective-permute-start | bytes 1204232 | tf_op jit(solution)/shard_map/ppermute | solution.py:237
  6.5 0.0 collective-permute-done.mate_ref
  6.5 1.0 %copy-done = bf16[32,6272]{1,0:T(8,128)(2,1)S(1)} copy-done((bf16[32,6272]{1,0:T(8,128)(2,1)S(1)}, bf16[32,6272]{1,0:T(8,128)(2,1)}, u32[]{:S(2)}) %copy-start) | copy-done | bytes 401432
  7.5 0.5 shard_map.83
  8.1 1.5 %collective-permute-start.1 = (bf16[16,6272]{1,0:T(8,128)(2,1)S(1)}, bf16[16,6272]{1,0:T(8,128)(2,1)S(1)}, u32[]{:S(2)}, u32[]{:S(2)}) collective-permute-start(bf16[16,6272]{1,0:T(8,128)(2,1)S(1)} %get-tuple-element.21), channel_id=1, source_target_pairs={{0,2},{1,3},{2,0},{3,1},{4,6},{5,7},{6,4},{7,5},{8,10},{9,11},{10,... | collective-permute-start | bytes 602120 | tf_op jit(solution)/shard_map/ppermute | solution.py:237
  9.6 1.6 %collective-permute-start.2 = (bf16[16,6272]{1,0:T(8,128)(2,1)S(1)}, bf16[16,6272]{1,0:T(8,128)(2,1)S(1)}, u32[]{:S(2)}, u32[]{:S(2)}) collective-permute-start(bf16[16,6272]{1,0:T(8,128)(2,1)S(1)} %get-tuple-element.22), channel_id=1, source_target_pairs={{0,4},{1,5},{2,6},{3,7},{4,0},{5,1},{6,2},{7,3},{8,12},{9,13},{10,... | collective-permute-start | bytes 602120 | tf_op jit(solution)/shard_map/ppermute | solution.py:237
  11.2 0.0 copy-start.4
  11.2 0.5 collective-permute-start.3
  11.7 13.7 %collective-permute-done.4.packed_ref = bf16[32,6272]{1,0:T(8,128)(2,1)S(1)} collective-permute-done((bf16[32,6272]{1,0:T(8,128)(2,1)}, bf16[32,6272]{1,0:T(8,128)(2,1)S(1)}, u32[]{:S(2)}, u32[]{:S(2)}) %collective-permute-start.4) | collective-permute-done | bytes 401440 | tf_op jit(solution)/shard_map/ppermute | solution.py:237
  25.4 0.0 collective-permute-done.1.refs_0_.refs_1_
  25.4 2.8 %collective-permute-done.3.refs_2_.refs_3_ = bf16[16,6272]{1,0:T(8,128)(2,1)S(1)} collective-permute-done((bf16[16,6272]{1,0:T(8,128)(2,1)S(1)}, bf16[16,6272]{1,0:T(8,128)(2,1)S(1)}, u32[]{:S(2)}, u32[]{:S(2)}) %collective-permute-start.3) | collective-permute-done | bytes 200736 | tf_op jit(solution)/shard_map/ppermute | solution.py:237
  28.2 0.5 shard_map.84
  28.7 15.3 %all_to_all.10 = bf16[8,8,6272]{2,1,0:T(8,128)(2,1)S(1)} all-to-all(bf16[8,8,6272]{2,1,0:T(8,128)(2,1)S(1)} %bitcast.10), channel_id=1, replica_groups={{0,1,2,3,4,5,6,7},{8,9,10,11,12,13,14,15},{16,17,18,19,20,21,22,23},{24..., dimensions={0} | all-to-all | bytes 1605632 | tf_op jit(solution)/shard_map/all_to_all | solution.py:250
  44.1 0.0 copy-start.2
  44.1 0.0 copy-start.3
  44.1 2.0 %shard_map.85 = (bf16[16,6144]{1,0:T(8,128)(2,1)S(1)}, bf16[16,6144]{1,0:T(8,128)(2,1)S(1)}, bf16[16,6144]{1,0:T(8,128)(2,1)S(1)}, bf16[16,6144]{1,0:T(8,128)(2,1)S(1)}, bf16[64,6144]{1,0:T(8,128)(2,1)S(1)}) custom-call(bf16[16,6272]{1,0:T(8,128)(2,1)S(1)} %get-tuple-element.20.refs_0_, bf16[16,6272]{1,0:T(8,128)(2,1)S(1)} %collective-permute-done.1.refs_0_.refs_1_, ...), custom_call_target="tpu_custom_call" | custom-call | bytes 17367552 | tf_op jit(solution)/shard_map/pallas_call | solution.py:226
  46.2 14.2 %all_to_all.11 = bf16[8,8,6144]{2,1,0:T(8,128)(2,1)S(1)} all-to-all(bf16[8,8,6144]{2,1,0:T(8,128)(2,1)S(1)} %bitcast.11), channel_id=1, replica_groups={{0,1,2,3,4,5,6,7},{8,9,10,11,12,13,14,15},{16,17,18,19,20,21,22,23},{24..., dimensions={0} | all-to-all | bytes 1572864 | tf_op jit(solution)/shard_map/all_to_all | solution.py:250
  60.3 0.3 shard_map.86
  60.7 1.5 %collective-permute-start.5 = (bf16[16,6144]{1,0:T(8,128)(2,1)S(1)}, bf16[16,6144]{1,0:T(8,128)(2,1)S(1)}, u32[]{:S(2)}, u32[]{:S(2)}) collective-permute-start(bf16[16,6144]{1,0:T(8,128)(2,1)S(1)} %get-tuple-element.29), channel_id=1, source_target_pairs={{0,2},{1,3},{2,0},{3,1},{4,6},{5,7},{6,4},{7,5},{8,10},{9,11},{10,... | collective-permute-start | bytes 589832 | tf_op jit(solution)/shard_map/ppermute | solution.py:237
  62.2 0.6 collective-permute-start.6
  62.8 1.4 %collective-permute-start.7 = (bf16[16,6144]{1,0:T(8,128)(2,1)S(1)}, bf16[16,6144]{1,0:T(8,128)(2,1)S(1)}, u32[]{:S(2)}, u32[]{:S(2)}) collective-permute-start(bf16[16,6144]{1,0:T(8,128)(2,1)S(1)} %get-tuple-element.31), channel_id=1, source_target_pairs={{0,6},{1,7},{2,4},{3,5},{4,2},{5,3},{6,0},{7,1},{8,14},{9,15},{10,... | collective-permute-start | bytes 589832 | tf_op jit(solution)/shard_map/ppermute | solution.py:237
  64.2 3.9 %collective-permute-start.9 = (bf16[32,6144]{1,0:T(8,128)(2,1)S(1)}, bf16[32,6144]{1,0:T(8,128)(2,1)S(1)}, u32[]{:S(2)}, u32[]{:S(2)}) collective-permute-start(bf16[32,6144]{1,0:T(8,128)(2,1)S(1)} %get-tuple-element.34), channel_id=1, source_target_pairs={{0,8},{1,9},{2,10},{3,11},{4,12},{5,13},{6,14},{7,15},{8,0},{9,1},... | collective-permute-start | bytes 1179656 | tf_op jit(solution)/shard_map/ppermute | solution.py:237
  68.1 0.0 collective-permute-done.5.refs_1_
  68.1 9.8 %collective-permute-done.6.refs_2_ = bf16[16,6144]{1,0:T(8,128)(2,1)S(1)} collective-permute-done((bf16[16,6144]{1,0:T(8,128)(2,1)S(1)}, bf16[16,6144]{1,0:T(8,128)(2,1)S(1)}, u32[]{:S(2)}, u32[]{:S(2)}) %collective-permute-start.6) | collective-permute-done | bytes 196640 | tf_op jit(solution)/shard_map/ppermute | solution.py:237
  77.9 2.3 %collective-permute-done.7.refs_3_ = bf16[16,6144]{1,0:T(8,128)(2,1)S(1)} collective-permute-done((bf16[16,6144]{1,0:T(8,128)(2,1)S(1)}, bf16[16,6144]{1,0:T(8,128)(2,1)S(1)}, u32[]{:S(2)}, u32[]{:S(2)}) %collective-permute-start.7) | collective-permute-done | bytes 196640 | tf_op jit(solution)/shard_map/ppermute | solution.py:237
  80.3 0.4 shard_map.87
  80.7 0.1 collective-permute-start.8
  80.8 4.0 %collective-permute-done.9.far_ref = bf16[32,6144]{1,0:T(8,128)(2,1)S(1)} collective-permute-done((bf16[32,6144]{1,0:T(8,128)(2,1)S(1)}, bf16[32,6144]{1,0:T(8,128)(2,1)S(1)}, u32[]{:S(2)}, u32[]{:S(2)}) %collective-permute-start.9) | collective-permute-done | bytes 393248 | tf_op jit(solution)/shard_map/ppermute | solution.py:237
  84.8 0.0 collective-permute-done.8.mate_ref
  84.8 1.2 %shard_map.88 = bf16[16,12288]{1,0:T(8,128)(2,1)} custom-call(bf16[32,6144]{1,0:T(8,128)(2,1)S(1)} %get-tuple-element.32.near_ref, bf16[32,6144]{1,0:T(8,128)(2,1)S(1)} %collective-permute-done.8.mate_ref, bf16[32,6144]{1,0:T(8,128)(2,1)S(1)} %collective-permute-done.9.far_ref, bf16[16,12288]{1,0:T(8,128)(2,1)S(1)} %copy-done.2, bf16[12288]{0:T(1024)(128)(2,1)S(1)} %copy-done.3), custom_call_target="tpu_custom_call" | custom-call | bytes 1990656 | tf_op jit(solution)/shard_map/pallas_call | solution.py:226
  (17 shorter events, 0.0 us)
Async XLA Ops:
  2.5 4.0 %collective-permute-start = (bf16[32,6272]{1,0:T(8,128)(2,1)}, bf16[32,6272]{1,0:T(8,128)(2,1)S(1)}, u32[]{:S(2)}, u32[]{:S(2)}) collective-permute-start(bf16[32,6272]{1,0:T(8,128)(2,1)} %shard_map.82.own_ref), channel_id=1, source_target_pairs={{0,1},{1,0},{2,3},{3,2},{4,5},{5,4},{6,7},{7,6},{8,9},{9,8},{10,11... | collective-permute-start | bytes 1204232 | tf_op jit(solution)/shard_map/ppermute | solution.py:237
  2.9 22.5 %collective-permute-start.4 = (bf16[32,6272]{1,0:T(8,128)(2,1)}, bf16[32,6272]{1,0:T(8,128)(2,1)S(1)}, u32[]{:S(2)}, u32[]{:S(2)}) collective-permute-start(bf16[32,6272]{1,0:T(8,128)(2,1)} %shard_map.82.own_ref), channel_id=1, source_target_pairs={{0,8},{1,9},{2,10},{3,11},{4,12},{5,13},{6,14},{7,15},{8,0},{9,1},... | collective-permute-start | bytes 1204232 | tf_op jit(solution)/shard_map/ppermute | solution.py:237
  6.5 1.0 %copy-start = (bf16[32,6272]{1,0:T(8,128)(2,1)S(1)}, bf16[32,6272]{1,0:T(8,128)(2,1)}, u32[]{:S(2)}) copy-start(bf16[32,6272]{1,0:T(8,128)(2,1)} %shard_map.82.own_ref) | copy-start | bytes 1204228
  8.1 17.3 %collective-permute-start.1 = (bf16[16,6272]{1,0:T(8,128)(2,1)S(1)}, bf16[16,6272]{1,0:T(8,128)(2,1)S(1)}, u32[]{:S(2)}, u32[]{:S(2)}) collective-permute-start(bf16[16,6272]{1,0:T(8,128)(2,1)S(1)} %get-tuple-element.21), channel_id=1, source_target_pairs={{0,2},{1,3},{2,0},{3,1},{4,6},{5,7},{6,4},{7,5},{8,10},{9,11},{10,... | collective-permute-start | bytes 602120 | tf_op jit(solution)/shard_map/ppermute | solution.py:237
  9.6 15.8 %collective-permute-start.2 = (bf16[16,6272]{1,0:T(8,128)(2,1)S(1)}, bf16[16,6272]{1,0:T(8,128)(2,1)S(1)}, u32[]{:S(2)}, u32[]{:S(2)}) collective-permute-start(bf16[16,6272]{1,0:T(8,128)(2,1)S(1)} %get-tuple-element.22), channel_id=1, source_target_pairs={{0,4},{1,5},{2,6},{3,7},{4,0},{5,1},{6,2},{7,3},{8,12},{9,13},{10,... | collective-permute-start | bytes 602120 | tf_op jit(solution)/shard_map/ppermute | solution.py:237
  11.2 32.9 %slice-start = ((s8[6291456]{0:T(1024)(128)(4,1)}), s8[4194304]{0:T(1024)(128)(4,1)S(1)}, s32[]{:S(2)}) async-start(s8[6291456]{0:T(1024)(128)(4,1)} %bitcast.4), calls=%async_computation.2 | async-start | bytes 8388608
  11.2 32.9 %slice-start.2 = ((s8[6291456]{0:T(1024)(128)(4,1)}), s8[4194304]{0:T(1024)(128)(4,1)S(1)}, s32[]{:S(2)}) async-start(s8[6291456]{0:T(1024)(128)(4,1)} %bitcast.6), calls=%async_computation.4 | async-start | bytes 8388608
  11.2 32.9 %slice-start.1 = ((s8[6291456]{0:T(1024)(128)(4,1)}), s8[2097152]{0:T(1024)(128)(4,1)S(1)}, s32[]{:S(2)}) async-start(s8[6291456]{0:T(1024)(128)(4,1)} %bitcast.4), calls=%async_computation.3 | async-start | bytes 4194304
  11.2 32.9 %slice-start.3 = ((s8[6291456]{0:T(1024)(128)(4,1)}), s8[2097152]{0:T(1024)(128)(4,1)S(1)}, s32[]{:S(2)}) async-start(s8[6291456]{0:T(1024)(128)(4,1)} %bitcast.6), calls=%async_computation.5 | async-start | bytes 4194304
  11.2 32.9 %copy-start.4 = (bf16[256]{0:T(256)(128)(2,1)S(1)}, bf16[256]{0:T(256)(128)(2,1)}, u32[]{:S(2)}) copy-start(bf16[256]{0:T(256)(128)(2,1)} %refs_6_.1) | copy-start | bytes 1540
  11.2 17.0 %collective-permute-start.3 = (bf16[16,6272]{1,0:T(8,128)(2,1)S(1)}, bf16[16,6272]{1,0:T(8,128)(2,1)S(1)}, u32[]{:S(2)}, u32[]{:S(2)}) collective-permute-start(bf16[16,6272]{1,0:T(8,128)(2,1)S(1)} %get-tuple-element.23), channel_id=1, source_target_pairs={{0,6},{1,7},{2,4},{3,5},{4,2},{5,3},{6,0},{7,1},{8,14},{9,15},{10,... | collective-permute-start | bytes 602120 | tf_op jit(solution)/shard_map/ppermute | solution.py:237
  44.1 36.2 %copy-start.1 = (bf16[32,6272]{1,0:T(8,128)(2,1)S(1)}, bf16[32,6272]{1,0:T(8,128)(2,1)}, u32[]{:S(2)}) copy-start(bf16[32,6272]{1,0:T(8,128)(2,1)} %shard_map.82.own_ref) | copy-start | bytes 1204228
  44.1 40.7 %copy-start.2 = (bf16[16,12288]{1,0:T(8,128)(2,1)S(1)}, bf16[16,12288]{1,0:T(8,128)(2,1)}, u32[]{:S(2)}) copy-start(bf16[16,12288]{1,0:T(8,128)(2,1)} %tokens_ref.3) | copy-start | bytes 1179652
  44.1 40.7 %copy-start.3 = (bf16[12288]{0:T(1024)(128)(2,1)S(1)}, bf16[12288]{0:T(1024)(128)(2,1)}, u32[]{:S(2)}) copy-start(bf16[12288]{0:T(1024)(128)(2,1)} %b_out_ref.1) | copy-start | bytes 73732
  60.7 7.5 %collective-permute-start.5 = (bf16[16,6144]{1,0:T(8,128)(2,1)S(1)}, bf16[16,6144]{1,0:T(8,128)(2,1)S(1)}, u32[]{:S(2)}, u32[]{:S(2)}) collective-permute-start(bf16[16,6144]{1,0:T(8,128)(2,1)S(1)} %get-tuple-element.29), channel_id=1, source_target_pairs={{0,2},{1,3},{2,0},{3,1},{4,6},{5,7},{6,4},{7,5},{8,10},{9,11},{10,... | collective-permute-start | bytes 589832 | tf_op jit(solution)/shard_map/ppermute | solution.py:237
  62.2 15.7 %collective-permute-start.6 = (bf16[16,6144]{1,0:T(8,128)(2,1)S(1)}, bf16[16,6144]{1,0:T(8,128)(2,1)S(1)}, u32[]{:S(2)}, u32[]{:S(2)}) collective-permute-start(bf16[16,6144]{1,0:T(8,128)(2,1)S(1)} %get-tuple-element.30), channel_id=1, source_target_pairs={{0,4},{1,5},{2,6},{3,7},{4,0},{5,1},{6,2},{7,3},{8,12},{9,13},{10,... | collective-permute-start | bytes 589832 | tf_op jit(solution)/shard_map/ppermute | solution.py:237
  62.8 17.5 %collective-permute-start.7 = (bf16[16,6144]{1,0:T(8,128)(2,1)S(1)}, bf16[16,6144]{1,0:T(8,128)(2,1)S(1)}, u32[]{:S(2)}, u32[]{:S(2)}) collective-permute-start(bf16[16,6144]{1,0:T(8,128)(2,1)S(1)} %get-tuple-element.31), channel_id=1, source_target_pairs={{0,6},{1,7},{2,4},{3,5},{4,2},{5,3},{6,0},{7,1},{8,14},{9,15},{10,... | collective-permute-start | bytes 589832 | tf_op jit(solution)/shard_map/ppermute | solution.py:237
  64.2 20.6 %collective-permute-start.9 = (bf16[32,6144]{1,0:T(8,128)(2,1)S(1)}, bf16[32,6144]{1,0:T(8,128)(2,1)S(1)}, u32[]{:S(2)}, u32[]{:S(2)}) collective-permute-start(bf16[32,6144]{1,0:T(8,128)(2,1)S(1)} %get-tuple-element.34), channel_id=1, source_target_pairs={{0,8},{1,9},{2,10},{3,11},{4,12},{5,13},{6,14},{7,15},{8,0},{9,1},... | collective-permute-start | bytes 1179656 | tf_op jit(solution)/shard_map/ppermute | solution.py:237
  80.7 4.1 %collective-permute-start.8 = (bf16[32,6144]{1,0:T(8,128)(2,1)S(1)}, bf16[32,6144]{1,0:T(8,128)(2,1)S(1)}, u32[]{:S(2)}, u32[]{:S(2)}) collective-permute-start(bf16[32,6144]{1,0:T(8,128)(2,1)S(1)} %get-tuple-element.33), channel_id=1, source_target_pairs={{0,1},{1,0},{2,3},{3,2},{4,5},{5,4},{6,7},{7,6},{8,9},{9,8},{10,11... | collective-permute-start | bytes 1179656 | tf_op jit(solution)/shard_map/ppermute | solution.py:237

commit v3 on v2

v3 whole, which is shorter than its diff:
```python
import functools

import jax
import jax.numpy as jnp
from jax import lax
from jax.experimental import pallas as pl
from jax.experimental.pallas import tpu as pltpu
from jax.sharding import PartitionSpec as P

BLK = 128
LANES = 128
SUB = 8
WIDTH = 512
MIB = 1024 * 1024
SELECT_COST = 10_000_000_000
BACK_CHUNKS = 1

epsilon = 1e-05


def iota(shape, axis):
    return lax.broadcasted_iota(jnp.int32, shape, axis)


def touches(ids, device, per_device, active):
    owner = (ids.astype(jnp.int32) + (per_device - 1)) // per_device - 1
    touched = jnp.zeros(device.shape, jnp.bool_)
    for a in range(active):
        touched = touched | (owner[:, a : a + 1] == device)
    return touched


def route_matrix(ids, chips, per_device, active):
    shape = (ids.shape[0], chips * SUB)
    wanted = iota(shape, 1) % SUB == iota(shape, 0) % SUB
    me = lax.axis_index("neuron")
    device = 2 * (me // 2 ^ iota(shape, 1) // SUB) + me % 2
    return jnp.where(touches(ids, device, per_device, active) & wanted, 1.0, 0.0)


def norm_kernel(active_ref, tokens_ref, gain_ref, bias_ref, out_ref, *, nodes):
    rows, features = tokens_ref.shape
    half = features // 2
    packed = 2 * rows
    requests, active = active_ref.shape
    total = jnp.zeros((rows, LANES), jnp.float32)
    for j in range(0, features, LANES):
        total += tokens_ref[:, j : j + LANES].astype(jnp.float32)
    mean = jnp.sum(total, axis=1, keepdims=True) / features
    total = jnp.zeros((rows, LANES), jnp.float32)
    for j in range(0, features, LANES):
        centred = tokens_ref[:, j : j + LANES].astype(jnp.float32) - mean
        total += centred * centred
    scale = lax.rsqrt(jnp.sum(total, axis=1, keepdims=True) / features + epsilon)
    shape = (packed, packed)
    slot, item = iota(shape, 0), iota(shape, 1)
    source = (slot % SUB // nodes) * rows + slot // SUB * nodes + slot % nodes
    pack = jnp.where(item == source, 1.0, 0.0).astype(jnp.bfloat16)

    def normed(start):
        centred = tokens_ref[:, start : start + WIDTH].astype(jnp.float32) - mean
        gain = gain_ref[start : start + WIDTH].astype(jnp.float32).reshape(1, WIDTH)
        bias = bias_ref[start : start + WIDTH].astype(jnp.float32).reshape(1, WIDTH)
        return (centred * scale * gain + bias).astype(jnp.bfloat16)

    for j in range(0, half, WIDTH):
        both = jnp.concatenate([normed(j), normed(half + j)], axis=0)
        out_ref[:, j : j + WIDTH] = jnp.dot(pack, both, preferred_element_type=jnp.float32).astype(jnp.bfloat16)
    request, lane = iota((packed, LANES), 0) // SUB, iota((packed, LANES), 1)
    ids = jnp.zeros((packed, LANES), jnp.int32)
    for r in range(requests):
        for a in range(active):
            ids = jnp.where((request == r) & (lane == a), active_ref[r, a] + 1, ids)
    out_ref[:, half:] = ids.astype(jnp.float32).astype(jnp.bfloat16)


def select_kernel(own_ids_ref, mate_ids_ref, own_ref, mate_ref, *refs, chips, per_device, active):
    out_refs = refs[-chips:]
    total = own_ref.shape[1]
    for s, (ids_ref, packed_ref) in enumerate(((own_ids_ref, own_ref), (mate_ids_ref, mate_ref))):
        ids = ids_ref[:, ids_ref.shape[1] - LANES :].astype(jnp.float32)
        chosen = route_matrix(ids, chips, per_device, active).T.astype(jnp.bfloat16)
        for j in range(0, total, WIDTH):
            span = slice(j, min(j + WIDTH, total))
            rows = jnp.dot(chosen, packed_ref[:, span], preferred_element_type=jnp.float32)
            for k, out_ref in enumerate(out_refs):
                out_ref[s * SUB : (s + 1) * SUB, span] = rows[k * SUB : (k + 1) * SUB].astype(jnp.bfloat16)


def neuron_kernel(*refs, nodes, chips, chunks):
    x_ref = refs[-1]
    in_refs = [refs[:chips], refs[chips : 2 * chips]]
    at = 2 * chips
    w_in_ref, b_in_ref, w_out_ref = refs[at : at + 3]
    out_refs = [refs[at + 3 + i * chips : at + 3 + (i + 1) * chips] for i in range(1 + chunks)]
    slots = x_ref.shape[0]
    features, units = w_in_ref.shape
    half = features // 2
    per_device = units // BLK
    depth = half // 4
    chunk = half // chunks
    near_rows = 2 * SUB * chips
    for k in range(chips):
        here = slice(2 * SUB * k, 2 * SUB * (k + 1))
        x_ref[here, :] = in_refs[0][k][...]
        here = slice(near_rows + 2 * SUB * k, near_rows + 2 * SUB * (k + 1))
        x_ref[here, :] = in_refs[1][k][...]
    sums = []
    for h in range(2):
        total = jnp.zeros((slots, units), jnp.float32)
        for at in range(0, half, depth):
            total += jnp.dot(
                x_ref[:, at : at + depth],
                w_in_ref[h * half + at : h * half + at + depth, :],
                preferred_element_type=jnp.float32,
            )
        sums.append(total)
    first, second = sums
    upper = iota((slots, 1), 0) % SUB < nodes
    preact = jnp.where(
        upper,
        first + pltpu.roll(second, slots - nodes, 0),
        second + pltpu.roll(first, nodes, 0),
    ) + b_in_ref[...].astype(jnp.float32).reshape(1, units)
    ids = x_ref[:, half : half + LANES].astype(jnp.float32).astype(jnp.int32)
    own = lax.axis_index("neuron") * per_device + 1
    hidden = []
    for b in range(per_device):
        flag = jnp.max(jnp.where(ids == own + b, 1.0, 0.0), axis=1, keepdims=True)
        hidden.append(jnp.maximum(preact[:, b * BLK : (b + 1) * BLK], 0.0) * flag)
    hidden = jnp.concatenate(hidden, axis=1).astype(jnp.bfloat16)
    for at in range(0, half, depth):
        lo = jnp.dot(hidden, w_out_ref[:, at : at + depth], preferred_element_type=jnp.float32)
        hi = jnp.dot(hidden, w_out_ref[:, half + at : half + at + depth], preferred_element_type=jnp.float32)
        both = jnp.where(upper, lo, hi).astype(jnp.bfloat16)
        c, offset = at // chunk, at % chunk
        for k in range(chips):
            out_refs[0][k][:, at : at + depth] = both[2 * SUB * k : 2 * SUB * (k + 1)]
            far = both[near_rows + 2 * SUB * k : near_rows + 2 * SUB * (k + 1)]
            out_refs[1 + c][k][:, offset : offset + depth] = far


def gather_kernel(own_ref, mate_ref, *refs, chips, per_device, active):
    back_refs, out_refs = refs[:chips], refs[-2:]
    half = back_refs[0].shape[1]
    for s, ids_ref in enumerate((own_ref, mate_ref)):
        ids = ids_ref[:, ids_ref.shape[1] - LANES :].astype(jnp.float32)
        spread = route_matrix(ids, chips, per_device, active).astype(jnp.bfloat16)
        for j in range(0, half, WIDTH):
            back = jnp.concatenate([ref[s * SUB : (s + 1) * SUB, j : j + WIDTH] for ref in back_refs], axis=0)
            part = jnp.dot(spread, back, preferred_element_type=jnp.float32)
            out_refs[s][:, j : j + WIDTH] = part.astype(jnp.bfloat16)


def copy_kernel(*refs):
    count = len(refs) // 2
    for part_ref, copy_ref in zip(refs[:count], refs[count + 1 :], strict=True):
        copy_ref[...] = part_ref[...]


def finish_kernel(near_ref, mate_ref, *refs, nodes):
    far_refs, (tokens_ref, b_out_ref, out_ref) = refs[:-3], refs[-3:]
    rows, features = tokens_ref.shape
    half = features // 2
    shape = (2 * rows, 2 * rows)
    item, slot = iota(shape, 0), iota(shape, 1)
    source = item % rows // nodes * SUB + item // rows * nodes + item % nodes
    unpack = jnp.where(slot == source, 1.0, 0.0).astype(jnp.bfloat16)
    chunk = half // len(far_refs)
    for j in range(0, half, WIDTH):
        far = far_refs[j // chunk][:, j % chunk : j % chunk + WIDTH]
        both = jnp.zeros((2 * rows, WIDTH), jnp.float32)
        for part in (near_ref[:, j : j + WIDTH], mate_ref[:, j : j + WIDTH], far):
            both += jnp.dot(unpack, part, preferred_element_type=jnp.float32)
        for h in range(2):
            at = h * half + j
            mixed = (
                tokens_ref[:, at : at + WIDTH].astype(jnp.float32)
                + both[h * rows : (h + 1) * rows]
                + b_out_ref[at : at + WIDTH].astype(jnp.float32).reshape(1, WIDTH)
            )
            out_ref[:, at : at + WIDTH] = mixed.astype(jnp.bfloat16)


def body(tokens, active, ln_gain, ln_bias, w_in, b_in, w_out, b_out):
    rows, features = tokens.shape
    requests, active_count = active.shape
    nodes = rows // requests
    units = w_in.shape[1]
    half = features // 2
    device_count = lax.axis_size("neuron")
    half_count = device_count // 2
    per_device = units // BLK
    packed = requests * SUB
    smem = pl.BlockSpec(memory_space=pltpu.SMEM)
    vmem = pl.BlockSpec(memory_space=pltpu.VMEM)
    hbm = pl.BlockSpec(memory_space=pl.ANY)
    chips = half_count // 2
    routing = dict(chips=chips, per_device=per_device, active=active_count)
    back_chunk = half // BACK_CHUNKS

    def call(kernel, shapes, in_specs, *operands, scratch=(), cost=0, limit=0):
        size = 2 * sum(rows * columns for rows, columns in shapes) + sum(x.size * 2 for x in operands)
        size += sum(2 * rows * columns for rows, columns in scratch)
        return pl.pallas_call(
            kernel,
            out_shape=[jax.ShapeDtypeStruct(shape, jnp.bfloat16) for shape in shapes],
            in_specs=in_specs,
            out_specs=[vmem] * len(shapes),
            scratch_shapes=[pltpu.VMEM(shape, jnp.bfloat16) for shape in scratch],
            compiler_params=pltpu.CompilerParams(vmem_limit_bytes=max(size + 8 * MIB, limit)),
            cost_estimate=pl.CostEstimate(flops=cost, bytes_accessed=size, transcendentals=0),
        )(*operands)

    def after(x, *others):
        return pl.pallas_call(
            lambda *refs: None,
            out_shape=jax.ShapeDtypeStruct(x.shape, x.dtype),
            in_specs=[hbm] * (1 + len(others)),
            out_specs=hbm,
            input_output_aliases={0: 0},
            compiler_params=pltpu.CompilerParams(vmem_limit_bytes=MIB),
            cost_estimate=pl.CostEstimate(flops=0, bytes_accessed=0, transcendentals=0),
        )(x, *others)

    def swap(x, partner):
        return lax.ppermute(x, "neuron", [(i, partner(i)) for i in range(device_count)])

    def across(x):
        return swap(x, lambda i: (i + half_count) % device_count)

    def mate_of(x):
        return swap(x, lambda i: i ^ 1)

    def to_chips(xs):
        return [xs[0]] + [swap(x, lambda i, k=k: i ^ 2 * k) for k, x in enumerate(xs) if k]

    def select(ids, packed_rows, order, cost):
        return call(
            functools.partial(select_kernel, **routing),
            [(2 * SUB, packed_rows[0].shape[1])] * chips,
            [vmem] * 4 + [hbm] * len(order),
            *ids, *packed_rows, *order,
            cost=cost,
        )

    def gather(ids, parts, order=()):
        back = to_chips(parts)
        return call(
            functools.partial(gather_kernel, **routing),
            [(packed, back[0].shape[1])] * 2,
            [vmem] * (2 + chips) + [hbm] * len(order),
            *ids, *back, *order,
        )

    [own] = call(
        functools.partial(norm_kernel, nodes=nodes),
        [(packed, half + LANES)],
        [smem, vmem, vmem, vmem],
        active, tokens, ln_gain, ln_bias,
        limit=56 * MIB,
    )
    other = across(own)
    near_ids = own, mate_of(own)
    near_rows = to_chips(select(near_ids, near_ids, (), 0))
    other = after(other, *near_rows[1:])
    far_ids = other, mate_of(other)
    far_rows = to_chips(select(far_ids, far_ids, (), SELECT_COST))
    parts = call(
        functools.partial(neuron_kernel, nodes=nodes, chips=chips, chunks=BACK_CHUNKS),
        [(2 * SUB, half)] * chips + [(2 * SUB, back_chunk)] * (chips * BACK_CHUNKS),
        [vmem] * (2 * chips + 3),
        *near_rows, *far_rows, w_in, b_in, w_out,
        scratch=[(2 * half_count * SUB, half + LANES)],
    )
    near_parts = parts[:chips]
    totals, far_sums = [], []
    for c in range(BACK_CHUNKS):
        kept, passed = gather(far_ids, parts[(1 + c) * chips : (2 + c) * chips])
        total = kept.astype(jnp.float32) + mate_of(passed).astype(jnp.float32)
        totals.append(total.astype(jnp.bfloat16))
        far_sums.append(across(totals[-1]))
    near_sent = call(
        copy_kernel,
        [(2 * SUB, half)] * (chips - 1),
        [vmem] * (chips - 1) + [hbm],
        *near_parts[1:], totals[-1],
    )
    near_kept, near_passed = gather(near_ids, [near_parts[0], *near_sent])
    [mixed] = call(
        functools.partial(finish_kernel, nodes=nodes),
        [(rows, features)],
        [vmem] * (4 + BACK_CHUNKS),
        near_kept, mate_of(near_passed), *far_sums, tokens, b_out,
    )
    return mixed


def solution(mesh):
    placed = (
        P(("groups", "neuron"), None),
        P(("groups", "neuron"), None),
        P(),
        P(),
        P(None, "neuron"),
        P("neuron"),
        P("neuron", None),
        P(),
    )
    return jax.shard_map(
        body, mesh=mesh, in_specs=placed, out_specs=P(("groups", "neuron"), None), check_vma=False
    )
```

time: 86.3 us -> 83.9 us (0.972)
  blocking collectives: 29.5 us -> 0 us
  waiting for transfers between devices: 32.7 us -> 53.3 us
  starting transfers between devices: 15.2 us -> 21.5 us
    all_to_all x2 -> x0, blocking collectives: 29.5 us -> none  [exchange(): lax.all_to_all(x.reshape(half_count, SUB, width), 'neuron', 0, 0, axis_in...]
    ppermute x10 -> x18, waiting for transfers between devices: 32.7 us -> 53.3 us  [swap(): lax.ppermute(x, 'neuron', [(i, partner(i)) for i in range(device_count)])]
    ppermute x10 -> x18, starting transfers between devices: 15.2 us -> 21.5 us  [swap(): lax.ppermute(x, 'neuron', [(i, partner(i)) for i in range(device_count)])]
    pallas_call x7 -> x8, Pallas kernels: 7.5 us -> 7.66 us  [call(): pl.pallas_call(kernel, out_shape=[jax.ShapeDtypeStruct(shape, jnp.bfloat1...]
  transfers between devices with their start and end apart: 10 -> 18, of which waited for: 5 -> 14; matrix products, arithmetic and copies ran while one was open for 0% -> 0% of each run, Pallas kernels for 1% -> 1%
where the time goes in v3:
time: 83.9 us; the launch traced here: 83.8 us
  waiting for transfers between devices  53.3 us (64%)
  starting transfers between devices  21.5 us (26%)
  Pallas kernels  7.66 us (9%)
  local copies, waits for them, and re-layouts  1.07 us (1%)
    ppermute x18, waiting for transfers between devices, swap(): lax.ppermute(x, 'neuron', [(i, partner(i)) for i in range(device_count)])  53.3 us
    ppermute x18, starting transfers between devices, swap(): lax.ppermute(x, 'neuron', [(i, partner(i)) for i in range(device_count)])  21.5 us
    pallas_call x8, Pallas kernels, call(): pl.pallas_call(kernel, out_shape=[jax.ShapeDtypeStruct(shape, jnp.bfloat1...  7.66 us
  transfers between devices with their start and end apart: 18, of which 14 were waited for; matrix products, arithmetic and copies ran while one was open for 0% of the time, Pallas kernels for 1%

profile of v3, /device:TPU:0, one launch (start us, length us, event | category | flops | bytes accessed | tf_op | source)
XLA Modules:
  0.0 83.8 jit_solution(14070309613578991509)
XLA Ops:
  0.0 2.5 %shard_map.82.own_ids_ref.own_ref = bf16[32,6272]{1,0:T(8,128)(2,1)} custom-call(s32[4,3]{1,0:T(4,128)} %active_ref.1, bf16[16,12288]{1,0:T(8,128)(2,1)} %refs_1_.1, bf16[12288]{0:T(1024)(128)(2,1)} %gain_ref.1, bf16[12288]{0:T(1024)(128)(2,1)} %bias_ref.1), custom_call_target="tpu_custom_call" | custom-call | bytes 843800 | tf_op jit(solution)/shard_map/pallas_call | solution.py:205
  2.5 0.5 collective-permute-start
  2.9 3.6 %collective-permute-start.4 = (bf16[32,6272]{1,0:T(8,128)(2,1)}, bf16[32,6272]{1,0:T(8,128)(2,1)S(1)}, u32[]{:S(2)}, u32[]{:S(2)}) collective-permute-start(bf16[32,6272]{1,0:T(8,128)(2,1)} %shard_map.82.own_ids_ref.own_ref), channel_id=1, source_target_pairs={{0,8},{1,9},{2,10},{3,11},{4,12},{5,13},{6,14},{7,15},{8,0},{9,1},... | collective-permute-start | bytes 1204232 | tf_op jit(solution)/shard_map/ppermute | solution.py:227
  6.5 1.0 %copy-done = bf16[32,6272]{1,0:T(8,128)(2,1)S(1)} copy-done((bf16[32,6272]{1,0:T(8,128)(2,1)S(1)}, bf16[32,6272]{1,0:T(8,128)(2,1)}, u32[]{:S(2)}) %copy-start) | copy-done | bytes 401432
  7.5 0.5 shard_map.83
  8.0 1.6 %collective-permute-start.1 = (bf16[16,6272]{1,0:T(8,128)(2,1)S(1)}, bf16[16,6272]{1,0:T(8,128)(2,1)S(1)}, u32[]{:S(2)}, u32[]{:S(2)}) collective-permute-start(bf16[16,6272]{1,0:T(8,128)(2,1)S(1)} %get-tuple-element.29), channel_id=1, source_target_pairs={{0,2},{1,3},{2,0},{3,1},{4,6},{5,7},{6,4},{7,5},{8,10},{9,11},{10,... | collective-permute-start | bytes 602120 | tf_op jit(solution)/shard_map/ppermute | solution.py:227
  9.6 1.6 %collective-permute-start.2 = (bf16[16,6272]{1,0:T(8,128)(2,1)S(1)}, bf16[16,6272]{1,0:T(8,128)(2,1)S(1)}, u32[]{:S(2)}, u32[]{:S(2)}) collective-permute-start(bf16[16,6272]{1,0:T(8,128)(2,1)S(1)} %get-tuple-element.30), channel_id=1, source_target_pairs={{0,4},{1,5},{2,6},{3,7},{4,0},{5,1},{6,2},{7,3},{8,12},{9,13},{10,... | collective-permute-start | bytes 602120 | tf_op jit(solution)/shard_map/ppermute | solution.py:227
  11.6 13.8 %collective-permute-done.4.refs_0_ = bf16[32,6272]{1,0:T(8,128)(2,1)S(1)} collective-permute-done((bf16[32,6272]{1,0:T(8,128)(2,1)}, bf16[32,6272]{1,0:T(8,128)(2,1)S(1)}, u32[]{:S(2)}, u32[]{:S(2)}) %collective-permute-start.4) | collective-permute-done | bytes 401440 | tf_op jit(solution)/shard_map/ppermute | solution.py:227
  25.4 2.8 %collective-permute-done.3.refs_3_ = bf16[16,6272]{1,0:T(8,128)(2,1)S(1)} collective-permute-done((bf16[16,6272]{1,0:T(8,128)(2,1)S(1)}, bf16[16,6272]{1,0:T(8,128)(2,1)S(1)}, u32[]{:S(2)}, u32[]{:S(2)}) %collective-permute-start.3) | collective-permute-done | bytes 200736 | tf_op jit(solution)/shard_map/ppermute | solution.py:227
  28.3 1.7 %collective-permute-done.5.mate_ids_ref.mate_ref = bf16[32,6272]{1,0:T(8,128)(2,1)S(1)} collective-permute-done((bf16[32,6272]{1,0:T(8,128)(2,1)S(1)}, bf16[32,6272]{1,0:T(8,128)(2,1)S(1)}, u32[]{:S(2)}, u32[]{:S(2)}) %collective-permute-start.5) | collective-permute-done | bytes 401440 | tf_op jit(solution)/shard_map/ppermute | solution.py:227
  30.1 0.5 shard_map.85
  30.6 1.5 %collective-permute-start.6 = (bf16[16,6272]{1,0:T(8,128)(2,1)S(1)}, bf16[16,6272]{1,0:T(8,128)(2,1)S(1)}, u32[]{:S(2)}, u32[]{:S(2)}) collective-permute-start(bf16[16,6272]{1,0:T(8,128)(2,1)S(1)} %get-tuple-element.33), channel_id=1, source_target_pairs={{0,2},{1,3},{2,0},{3,1},{4,6},{5,7},{6,4},{7,5},{8,10},{9,11},{10,... | collective-permute-start | bytes 602120 | tf_op jit(solution)/shard_map/ppermute | solution.py:227
  32.0 2.1 %collective-permute-start.8 = (bf16[16,6272]{1,0:T(8,128)(2,1)S(1)}, bf16[16,6272]{1,0:T(8,128)(2,1)S(1)}, u32[]{:S(2)}, u32[]{:S(2)}) collective-permute-start(bf16[16,6272]{1,0:T(8,128)(2,1)S(1)} %get-tuple-element.35), channel_id=1, source_target_pairs={{0,6},{1,7},{2,4},{3,5},{4,2},{5,3},{6,0},{7,1},{8,14},{9,15},{10,... | collective-permute-start | bytes 602120 | tf_op jit(solution)/shard_map/ppermute | solution.py:227
  34.1 3.5 %collective-permute-done.6.refs_5_ = bf16[16,6272]{1,0:T(8,128)(2,1)S(1)} collective-permute-done((bf16[16,6272]{1,0:T(8,128)(2,1)S(1)}, bf16[16,6272]{1,0:T(8,128)(2,1)S(1)}, u32[]{:S(2)}, u32[]{:S(2)}) %collective-permute-start.6) | collective-permute-done | bytes 200736 | tf_op jit(solution)/shard_map/ppermute | solution.py:227
  37.7 2.3 %collective-permute-done.7.refs_6_ = bf16[16,6272]{1,0:T(8,128)(2,1)S(1)} collective-permute-done((bf16[16,6272]{1,0:T(8,128)(2,1)S(1)}, bf16[16,6272]{1,0:T(8,128)(2,1)S(1)}, u32[]{:S(2)}, u32[]{:S(2)}) %collective-permute-start.7) | collective-permute-done | bytes 200736 | tf_op jit(solution)/shard_map/ppermute | solution.py:227
  39.9 3.2 %collective-permute-done.8.refs_7_ = bf16[16,6272]{1,0:T(8,128)(2,1)S(1)} collective-permute-done((bf16[16,6272]{1,0:T(8,128)(2,1)S(1)}, bf16[16,6272]{1,0:T(8,128)(2,1)S(1)}, u32[]{:S(2)}, u32[]{:S(2)}) %collective-permute-start.8) | collective-permute-done | bytes 200736 | tf_op jit(solution)/shard_map/ppermute | solution.py:227
  43.2 2.1 %shard_map.86 = (bf16[16,6144]{1,0:T(8,128)(2,1)S(1)}, bf16[16,6144]{1,0:T(8,128)(2,1)S(1)}, bf16[16,6144]{1,0:T(8,128)(2,1)S(1)}, bf16[16,6144]{1,0:T(8,128)(2,...) custom-call(bf16[16,6272]{1,0:T(8,128)(2,1)S(1)} %get-tuple-element., ...), custom_call_target="tpu_custom_call" | custom-call | bytes 17367552 | tf_op jit(solution)/shard_map/pallas_call | solution.py:205
  45.3 1.5 %collective-permute-start.9 = (bf16[16,6144]{1,0:T(8,128)(2,1)S(1)}, bf16[16,6144]{1,0:T(8,128)(2,1)S(1)}, u32[]{:S(2)}, u32[]{:S(2)}) collective-permute-start(bf16[16,6144]{1,0:T(8,128)(2,1)S(1)} %get-tuple-element.41), channel_id=1, source_target_pairs={{0,2},{1,3},{2,0},{3,1},{4,6},{5,7},{6,4},{7,5},{8,10},{9,11},{10,... | collective-permute-start | bytes 589832 | tf_op jit(solution)/shard_map/ppermute | solution.py:227
  47.1 1.8 %collective-permute-start.11 = (bf16[16,6144]{1,0:T(8,128)(2,1)S(1)}, bf16[16,6144]{1,0:T(8,128)(2,1)S(1)}, u32[]{:S(2)}, u32[]{:S(2)}) collective-permute-start(bf16[16,6144]{1,0:T(8,128)(2,1)S(1)} %get-tuple-element.43), channel_id=1, source_target_pairs={{0,6},{1,7},{2,4},{3,5},{4,2},{5,3},{6,0},{7,1},{8,14},{9,15},{10,... | collective-permute-start | bytes 589832 | tf_op jit(solution)/shard_map/ppermute | solution.py:227
  48.8 3.4 %collective-permute-done.9.refs_1_ = bf16[16,6144]{1,0:T(8,128)(2,1)S(1)} collective-permute-done((bf16[16,6144]{1,0:T(8,128)(2,1)S(1)}, bf16[16,6144]{1,0:T(8,128)(2,1)S(1)}, u32[]{:S(2)}, u32[]{:S(2)}) %collective-permute-start.9) | collective-permute-done | bytes 196640 | tf_op jit(solution)/shard_map/ppermute | solution.py:227
  52.3 2.1 %collective-permute-done.10.refs_2_ = bf16[16,6144]{1,0:T(8,128)(2,1)S(1)} collective-permute-done((bf16[16,6144]{1,0:T(8,128)(2,1)S(1)}, bf16[16,6144]{1,0:T(8,128)(2,1)S(1)}, u32[]{:S(2)}, u32[]{:S(2)}) %collective-permute-start.10) | collective-permute-done | bytes 196640 | tf_op jit(solution)/shard_map/ppermute | solution.py:227
  54.4 2.1 %collective-permute-done.11.refs_3_ = bf16[16,6144]{1,0:T(8,128)(2,1)S(1)} collective-permute-done((bf16[16,6144]{1,0:T(8,128)(2,1)S(1)}, bf16[16,6144]{1,0:T(8,128)(2,1)S(1)}, u32[]{:S(2)}, u32[]{:S(2)}) %collective-permute-start.11) | collective-permute-done | bytes 196640 | tf_op jit(solution)/shard_map/ppermute | solution.py:227
  56.5 0.4 shard_map.87
  57.0 1.7 %collective-permute-done.12 = bf16[32,6144]{1,0:T(8,128)(2,1)S(1)} collective-permute-done((bf16[32,6144]{1,0:T(8,128)(2,1)S(1)}, bf16[32,6144]{1,0:T(8,128)(2,1)S(1)}, u32[]{:S(2)}, u32[]{:S(2)}) %collective-permute-start.12) | collective-permute-done | bytes 393248 | tf_op jit(solution)/shard_map/ppermute | solution.py:227
  58.9 1.5 %collective-permute-start.13 = (bf16[16,6144]{1,0:T(8,128)(2,1)S(1)}, bf16[16,6144]{1,0:T(8,128)(2,1)S(1)}, u32[]{:S(2)}, u32[]{:S(2)}) collective-permute-start(bf16[16,6144]{1,0:T(8,128)(2,1)S(1)} %get-tuple-element.46), channel_id=1, source_target_pairs={{0,2},{1,3},{2,0},{3,1},{4,6},{5,7},{6,4},{7,5},{8,10},{9,11},{10,... | collective-permute-start | bytes 589832 | tf_op jit(solution)/shard_map/ppermute | solution.py:227
  60.4 0.6 collective-permute-start.14
  61.0 1.4 %collective-permute-start.15 = (bf16[16,6144]{1,0:T(8,128)(2,1)S(1)}, bf16[16,6144]{1,0:T(8,128)(2,1)S(1)}, u32[]{:S(2)}, u32[]{:S(2)}) collective-permute-start(bf16[16,6144]{1,0:T(8,128)(2,1)S(1)} %get-tuple-element.48), channel_id=1, source_target_pairs={{0,6},{1,7},{2,4},{3,5},{4,2},{5,3},{6,0},{7,1},{8,14},{9,15},{10,... | collective-permute-start | bytes 589832 | tf_op jit(solution)/shard_map/ppermute | solution.py:227
  62.5 3.0 %collective-permute-start.17 = (bf16[32,6144]{1,0:T(8,128)(2,1)S(1)}, bf16[32,6144]{1,0:T(8,128)(2,1)S(1)}, u32[]{:S(2)}, u32[]{:S(2)}) collective-permute-start(bf16[32,6144]{1,0:T(8,128)(2,1)S(1)} %add_convert_fusion.refs_3_), channel_id=1, source_target_pairs={{0,8},{1,9},{2,10},{3,11},{4,12},{5,13},{6,14},{7,15},{8,0},{9,1},... | collective-permute-start | bytes 1179656 | tf_op jit(solution)/shard_map/ppermute | solution.py:227
  65.9 10.4 %collective-permute-done.14.refs_2_ = bf16[16,6144]{1,0:T(8,128)(2,1)S(1)} collective-permute-done((bf16[16,6144]{1,0:T(8,128)(2,1)S(1)}, bf16[16,6144]{1,0:T(8,128)(2,1)S(1)}, u32[]{:S(2)}, u32[]{:S(2)}) %collective-permute-start.14) | collective-permute-done | bytes 196640 | tf_op jit(solution)/shard_map/ppermute | solution.py:227
  76.3 2.3 %collective-permute-done.15.refs_3_ = bf16[16,6144]{1,0:T(8,128)(2,1)S(1)} collective-permute-done((bf16[16,6144]{1,0:T(8,128)(2,1)S(1)}, bf16[16,6144]{1,0:T(8,128)(2,1)S(1)}, u32[]{:S(2)}, u32[]{:S(2)}) %collective-permute-start.15) | collective-permute-done | bytes 196640 | tf_op jit(solution)/shard_map/ppermute | solution.py:227
  79.1 3.4 %collective-permute-done.17.refs_0_ = bf16[32,6144]{1,0:T(8,128)(2,1)S(1)} collective-permute-done((bf16[32,6144]{1,0:T(8,128)(2,1)S(1)}, bf16[32,6144]{1,0:T(8,128)(2,1)S(1)}, u32[]{:S(2)}, u32[]{:S(2)}) %collective-permute-start.17) | collective-permute-done | bytes 393248 | tf_op jit(solution)/shard_map/ppermute | solution.py:227
  82.5 1.2 %shard_map.90 = bf16[16,12288]{1,0:T(8,128)(2,1)} custom-call(bf16[32,6144]{1,0:T(8,128)(2,1)S(1)} %get-tuple-element.49.near_ref, bf16[32,6144]{1,0:T(8,128)(2,1)S(1)} %collective-permute-done.16.mate_ref, bf16[32,6144]{1,0:T(8,128)(2,1)S(1)} %collective-permute-done.17.refs_0_, bf16[16,12288]{1,0:T(8,128)(2,1)S(1)} %copy-done.2, bf16[12288]{0:T(1024)(128)(2,1)S(1)} %copy-done.3), custom_call_target="tpu_custom_call" | custom-call | bytes 1990656 | tf_op jit(solution)/shard_map/pallas_call | solution.py:205
  (34 shorter events, 1.9 us)
Async XLA Ops:
  2.5 4.0 %collective-permute-start = (bf16[32,6272]{1,0:T(8,128)(2,1)}, bf16[32,6272]{1,0:T(8,128)(2,1)S(1)}, u32[]{:S(2)}, u32[]{:S(2)}) collective-permute-start(bf16[32,6272]{1,0:T(8,128)(2,1)} %shard_map.82.own_ids_ref.own_ref), channel_id=1, source_target_pairs={{0,1},{1,0},{2,3},{3,2},{4,5},{5,4},{6,7},{7,6},{8,9},{9,8},{10,11... | collective-permute-start | bytes 1204232 | tf_op jit(solution)/shard_map/ppermute | solution.py:227
  2.9 22.5 %collective-permute-start.4 = (bf16[32,6272]{1,0:T(8,128)(2,1)}, bf16[32,6272]{1,0:T(8,128)(2,1)S(1)}, u32[]{:S(2)}, u32[]{:S(2)}) collective-permute-start(bf16[32,6272]{1,0:T(8,128)(2,1)} %shard_map.82.own_ids_ref.own_ref), channel_id=1, source_target_pairs={{0,8},{1,9},{2,10},{3,11},{4,12},{5,13},{6,14},{7,15},{8,0},{9,1},... | collective-permute-start | bytes 1204232 | tf_op jit(solution)/shard_map/ppermute | solution.py:227
  6.5 1.0 %copy-start = (bf16[32,6272]{1,0:T(8,128)(2,1)S(1)}, bf16[32,6272]{1,0:T(8,128)(2,1)}, u32[]{:S(2)}) copy-start(bf16[32,6272]{1,0:T(8,128)(2,1)} %shard_map.82.own_ids_ref.own_ref) | copy-start | bytes 1204228
  8.0 17.3 %collective-permute-start.1 = (bf16[16,6272]{1,0:T(8,128)(2,1)S(1)}, bf16[16,6272]{1,0:T(8,128)(2,1)S(1)}, u32[]{:S(2)}, u32[]{:S(2)}) collective-permute-start(bf16[16,6272]{1,0:T(8,128)(2,1)S(1)} %get-tuple-element.29), channel_id=1, source_target_pairs={{0,2},{1,3},{2,0},{3,1},{4,6},{5,7},{6,4},{7,5},{8,10},{9,11},{10,... | collective-permute-start | bytes 602120 | tf_op jit(solution)/shard_map/ppermute | solution.py:227
  9.6 15.8 %collective-permute-start.2 = (bf16[16,6272]{1,0:T(8,128)(2,1)S(1)}, bf16[16,6272]{1,0:T(8,128)(2,1)S(1)}, u32[]{:S(2)}, u32[]{:S(2)}) collective-permute-start(bf16[16,6272]{1,0:T(8,128)(2,1)S(1)} %get-tuple-element.30), channel_id=1, source_target_pairs={{0,4},{1,5},{2,6},{3,7},{4,0},{5,1},{6,2},{7,3},{8,12},{9,13},{10,... | collective-permute-start | bytes 602120 | tf_op jit(solution)/shard_map/ppermute | solution.py:227
  11.2 17.1 %collective-permute-start.3 = (bf16[16,6272]{1,0:T(8,128)(2,1)S(1)}, bf16[16,6272]{1,0:T(8,128)(2,1)S(1)}, u32[]{:S(2)}, u32[]{:S(2)}) collective-permute-start(bf16[16,6272]{1,0:T(8,128)(2,1)S(1)} %get-tuple-element.31), channel_id=1, source_target_pairs={{0,6},{1,7},{2,4},{3,5},{4,2},{5,3},{6,0},{7,1},{8,14},{9,15},{10,... | collective-permute-start | bytes 602120 | tf_op jit(solution)/shard_map/ppermute | solution.py:227
  28.2 14.9 %slice-start = ((s8[6291456]{0:T(1024)(128)(4,1)}), s8[4194304]{0:T(1024)(128)(4,1)S(1)}, s32[]{:S(2)}) async-start(s8[6291456]{0:T(1024)(128)(4,1)} %bitcast), calls=%async_computation | async-start | bytes 8388608
  28.2 14.9 %slice-start.2 = ((s8[6291456]{0:T(1024)(128)(4,1)}), s8[4194304]{0:T(1024)(128)(4,1)S(1)}, s32[]{:S(2)}) async-start(s8[6291456]{0:T(1024)(128)(4,1)} %bitcast.2), calls=%async_computation.2 | async-start | bytes 8388608
  28.2 14.9 %slice-start.1 = ((s8[6291456]{0:T(1024)(128)(4,1)}), s8[2097152]{0:T(1024)(128)(4,1)S(1)}, s32[]{:S(2)}) async-start(s8[6291456]{0:T(1024)(128)(4,1)} %bitcast), calls=%async_computation.1 | async-start | bytes 4194304
  28.2 14.9 %slice-start.3 = ((s8[6291456]{0:T(1024)(128)(4,1)}), s8[2097152]{0:T(1024)(128)(4,1)S(1)}, s32[]{:S(2)}) async-start(s8[6291456]{0:T(1024)(128)(4,1)} %bitcast.2), calls=%async_computation.3 | async-start | bytes 4194304
  28.2 14.9 %copy-start.4 = (bf16[256]{0:T(256)(128)(2,1)S(1)}, bf16[256]{0:T(256)(128)(2,1)}, u32[]{:S(2)}) copy-start(bf16[256]{0:T(256)(128)(2,1)} %refs_9_.1) | copy-start | bytes 1540
  28.3 1.8 %collective-permute-start.5 = (bf16[32,6272]{1,0:T(8,128)(2,1)S(1)}, bf16[32,6272]{1,0:T(8,128)(2,1)S(1)}, u32[]{:S(2)}, u32[]{:S(2)}) collective-permute-start(bf16[32,6272]{1,0:T(8,128)(2,1)S(1)} %shard_map.84.own_ids_ref.own_ref), channel_id=1, source_target_pairs={{0,1},{1,0},{2,3},{3,2},{4,5},{5,4},{6,7},{7,6},{8,9},{9,8},{10,11... | collective-permute-start | bytes 1204232 | tf_op jit(solution)/shard_map/ppermute | solution.py:227
  30.6 7.1 %collective-permute-start.6 = (bf16[16,6272]{1,0:T(8,128)(2,1)S(1)}, bf16[16,6272]{1,0:T(8,128)(2,1)S(1)}, u32[]{:S(2)}, u32[]{:S(2)}) collective-permute-start(bf16[16,6272]{1,0:T(8,128)(2,1)S(1)} %get-tuple-element.33), channel_id=1, source_target_pairs={{0,2},{1,3},{2,0},{3,1},{4,6},{5,7},{6,4},{7,5},{8,10},{9,11},{10,... | collective-permute-start | bytes 602120 | tf_op jit(solution)/shard_map/ppermute | solution.py:227
  32.0 7.9 %collective-permute-start.7 = (bf16[16,6272]{1,0:T(8,128)(2,1)S(1)}, bf16[16,6272]{1,0:T(8,128)(2,1)S(1)}, u32[]{:S(2)}, u32[]{:S(2)}) collective-permute-start(bf16[16,6272]{1,0:T(8,128)(2,1)S(1)} %get-tuple-element.34), channel_id=1, source_target_pairs={{0,4},{1,5},{2,6},{3,7},{4,0},{5,1},{6,2},{7,3},{8,12},{9,13},{10,... | collective-permute-start | bytes 602120 | tf_op jit(solution)/shard_map/ppermute | solution.py:227
  32.0 11.1 %collective-permute-start.8 = (bf16[16,6272]{1,0:T(8,128)(2,1)S(1)}, bf16[16,6272]{1,0:T(8,128)(2,1)S(1)}, u32[]{:S(2)}, u32[]{:S(2)}) collective-permute-start(bf16[16,6272]{1,0:T(8,128)(2,1)S(1)} %get-tuple-element.35), channel_id=1, source_target_pairs={{0,6},{1,7},{2,4},{3,5},{4,2},{5,3},{6,0},{7,1},{8,14},{9,15},{10,... | collective-permute-start | bytes 602120 | tf_op jit(solution)/shard_map/ppermute | solution.py:227
  43.2 35.4 %copy-start.1 = (bf16[32,6272]{1,0:T(8,128)(2,1)S(1)}, bf16[32,6272]{1,0:T(8,128)(2,1)}, u32[]{:S(2)}) copy-start(bf16[32,6272]{1,0:T(8,128)(2,1)} %shard_map.82.own_ids_ref.own_ref) | copy-start | bytes 1204228
  43.2 39.3 %copy-start.2 = (bf16[16,12288]{1,0:T(8,128)(2,1)S(1)}, bf16[16,12288]{1,0:T(8,128)(2,1)}, u32[]{:S(2)}) copy-start(bf16[16,12288]{1,0:T(8,128)(2,1)} %refs_1_.1) | copy-start | bytes 1179652
  43.2 39.3 %copy-start.3 = (bf16[12288]{0:T(1024)(128)(2,1)S(1)}, bf16[12288]{0:T(1024)(128)(2,1)}, u32[]{:S(2)}) copy-start(bf16[12288]{0:T(1024)(128)(2,1)} %refs_2_.1) | copy-start | bytes 73732
  45.3 7.0 %collective-permute-start.9 = (bf16[16,6144]{1,0:T(8,128)(2,1)S(1)}, bf16[16,6144]{1,0:T(8,128)(2,1)S(1)}, u32[]{:S(2)}, u32[]{:S(2)}) collective-permute-start(bf16[16,6144]{1,0:T(8,128)(2,1)S(1)} %get-tuple-element.41), channel_id=1, source_target_pairs={{0,2},{1,3},{2,0},{3,1},{4,6},{5,7},{6,4},{7,5},{8,10},{9,11},{10,... | collective-permute-start | bytes 589832 | tf_op jit(solution)/shard_map/ppermute | solution.py:227
  46.8 7.6 %collective-permute-start.10 = (bf16[16,6144]{1,0:T(8,128)(2,1)S(1)}, bf16[16,6144]{1,0:T(8,128)(2,1)S(1)}, u32[]{:S(2)}, u32[]{:S(2)}) collective-permute-start(bf16[16,6144]{1,0:T(8,128)(2,1)S(1)} %get-tuple-element.42), channel_id=1, source_target_pairs={{0,4},{1,5},{2,6},{3,7},{4,0},{5,1},{6,2},{7,3},{8,12},{9,13},{10,... | collective-permute-start | bytes 589832 | tf_op jit(solution)/shard_map/ppermute | solution.py:227
  47.1 9.5 %collective-permute-start.11 = (bf16[16,6144]{1,0:T(8,128)(2,1)S(1)}, bf16[16,6144]{1,0:T(8,128)(2,1)S(1)}, u32[]{:S(2)}, u32[]{:S(2)}) collective-permute-start(bf16[16,6144]{1,0:T(8,128)(2,1)S(1)} %get-tuple-element.43), channel_id=1, source_target_pairs={{0,6},{1,7},{2,4},{3,5},{4,2},{5,3},{6,0},{7,1},{8,14},{9,15},{10,... | collective-permute-start | bytes 589832 | tf_op jit(solution)/shard_map/ppermute | solution.py:227
  57.0 1.8 %collective-permute-start.12 = (bf16[32,6144]{1,0:T(8,128)(2,1)S(1)}, bf16[32,6144]{1,0:T(8,128)(2,1)S(1)}, u32[]{:S(2)}, u32[]{:S(2)}) collective-permute-start(bf16[32,6144]{1,0:T(8,128)(2,1)S(1)} %get-tuple-element.45), channel_id=1, source_target_pairs={{0,1},{1,0},{2,3},{3,2},{4,5},{5,4},{6,7},{7,6},{8,9},{9,8},{10,11... | collective-permute-start | bytes 1179656 | tf_op jit(solution)/shard_map/ppermute | solution.py:227
  58.9 7.0 %collective-permute-start.13 = (bf16[16,6144]{1,0:T(8,128)(2,1)S(1)}, bf16[16,6144]{1,0:T(8,128)(2,1)S(1)}, u32[]{:S(2)}, u32[]{:S(2)}) collective-permute-start(bf16[16,6144]{1,0:T(8,128)(2,1)S(1)} %get-tuple-element.46), channel_id=1, source_target_pairs={{0,2},{1,3},{2,0},{3,1},{4,6},{5,7},{6,4},{7,5},{8,10},{9,11},{10,... | collective-permute-start | bytes 589832 | tf_op jit(solution)/shard_map/ppermute | solution.py:227
  60.4 16.0 %collective-permute-start.14 = (bf16[16,6144]{1,0:T(8,128)(2,1)S(1)}, bf16[16,6144]{1,0:T(8,128)(2,1)S(1)}, u32[]{:S(2)}, u32[]{:S(2)}) collective-permute-start(bf16[16,6144]{1,0:T(8,128)(2,1)S(1)} %get-tuple-element.47), channel_id=1, source_target_pairs={{0,4},{1,5},{2,6},{3,7},{4,0},{5,1},{6,2},{7,3},{8,12},{9,13},{10,... | collective-permute-start | bytes 589832 | tf_op jit(solution)/shard_map/ppermute | solution.py:227
  61.0 17.6 %collective-permute-start.15 = (bf16[16,6144]{1,0:T(8,128)(2,1)S(1)}, bf16[16,6144]{1,0:T(8,128)(2,1)S(1)}, u32[]{:S(2)}, u32[]{:S(2)}) collective-permute-start(bf16[16,6144]{1,0:T(8,128)(2,1)S(1)} %get-tuple-element.48), channel_id=1, source_target_pairs={{0,6},{1,7},{2,4},{3,5},{4,2},{5,3},{6,0},{7,1},{8,14},{9,15},{10,... | collective-permute-start | bytes 589832 | tf_op jit(solution)/shard_map/ppermute | solution.py:227
  62.5 20.1 %collective-permute-start.17 = (bf16[32,6144]{1,0:T(8,128)(2,1)S(1)}, bf16[32,6144]{1,0:T(8,128)(2,1)S(1)}, u32[]{:S(2)}, u32[]{:S(2)}) collective-permute-start(bf16[32,6144]{1,0:T(8,128)(2,1)S(1)} %add_convert_fusion.refs_3_), channel_id=1, source_target_pairs={{0,8},{1,9},{2,10},{3,11},{4,12},{5,13},{6,14},{7,15},{8,0},{9,1},... | collective-permute-start | bytes 1179656 | tf_op jit(solution)/shard_map/ppermute | solution.py:227
  79.1 3.5 %collective-permute-start.16 = (bf16[32,6144]{1,0:T(8,128)(2,1)S(1)}, bf16[32,6144]{1,0:T(8,128)(2,1)S(1)}, u32[]{:S(2)}, u32[]{:S(2)}) collective-permute-start(bf16[32,6144]{1,0:T(8,128)(2,1)S(1)} %get-tuple-element.50), channel_id=1, source_target_pairs={{0,1},{1,0},{2,3},{3,2},{4,5},{5,4},{6,7},{7,6},{8,9},{9,8},{10,11... | collective-permute-start | bytes 1179656 | tf_op jit(solution)/shard_map/ppermute | solution.py:227

commit v4 on v3

--- a/solution.py
+++ b/solution.py
@@ -13,7 +13,6 @@
 WIDTH = 512
 MIB = 1024 * 1024
 SELECT_COST = 10_000_000_000
-BACK_CHUNKS = 1
 
 epsilon = 1e-05
 
@@ -87,18 +86,17 @@
                 out_ref[s * SUB : (s + 1) * SUB, span] = rows[k * SUB : (k + 1) * SUB].astype(jnp.bfloat16)
 
 
-def neuron_kernel(*refs, nodes, chips, chunks):
+def neuron_kernel(*refs, nodes, chips):
     x_ref = refs[-1]
     in_refs = [refs[:chips], refs[chips : 2 * chips]]
     at = 2 * chips
     w_in_ref, b_in_ref, w_out_ref = refs[at : at + 3]
-    out_refs = [refs[at + 3 + i * chips : at + 3 + (i + 1) * chips] for i in range(1 + chunks)]
+    near_out_refs, far_out_refs = refs[at + 3 : at + 5], refs[at + 5 : -1]
     slots = x_ref.shape[0]
     features, units = w_in_ref.shape
     half = features // 2
     per_device = units // BLK
     depth = half // 4
-    chunk = half // chunks
     near_rows = 2 * SUB * chips
     for k in range(chips):
         here = slice(2 * SUB * k, 2 * SUB * (k + 1))
@@ -133,11 +131,12 @@
         lo = jnp.dot(hidden, w_out_ref[:, at : at + depth], preferred_element_type=jnp.float32)
         hi = jnp.dot(hidden, w_out_ref[:, half + at : half + at + depth], preferred_element_type=jnp.float32)
         both = jnp.where(upper, lo, hi).astype(jnp.bfloat16)
-        c, offset = at // chunk, at % chunk
         for k in range(chips):
-            out_refs[0][k][:, at : at + depth] = both[2 * SUB * k : 2 * SUB * (k + 1)]
+            for s, near_out_ref in enumerate(near_out_refs):
+                slot = both[(2 * k + s) * SUB : (2 * k + s + 1) * SUB]
+                near_out_ref[k * SUB : (k + 1) * SUB, at : at + depth] = slot
             far = both[near_rows + 2 * SUB * k : near_rows + 2 * SUB * (k + 1)]
-            out_refs[1 + c][k][:, offset : offset + depth] = far
+            far_out_refs[k][:, at : at + depth] = far
 
 
 def gather_kernel(own_ref, mate_ref, *refs, chips, per_device, active):
@@ -152,26 +151,41 @@
             out_refs[s][:, j : j + WIDTH] = part.astype(jnp.bfloat16)
 
 
-def copy_kernel(*refs):
-    count = len(refs) // 2
-    for part_ref, copy_ref in zip(refs[:count], refs[count + 1 :], strict=True):
-        copy_ref[...] = part_ref[...]
-
-
-def finish_kernel(near_ref, mate_ref, *refs, nodes):
-    far_refs, (tokens_ref, b_out_ref, out_ref) = refs[:-3], refs[-3:]
+def pair_kernel(kept_ref, received_ref, *refs, places):
+    for k, out_ref in zip(places, refs[-len(places) :], strict=True):
+        for s, ref in enumerate((kept_ref, received_ref)):
+            out_ref[s * SUB : (s + 1) * SUB, :] = ref[k * SUB : (k + 1) * SUB, :]
+
+
+def plan_kernel(active_ref, order_ref, out_ref, *, rows, nodes, near_rows, per_device):
+    requests, active = active_ref.shape
+    me = lax.axis_index("neuron")
+
+    def match(cols):
+        shape = (2 * rows, cols)
+        item, slot = iota(shape, 0), iota(shape, 1)
+        return item % rows // nodes, slot // SUB, slot % SUB == item // rows * nodes + item % nodes
+
+    request, place, aligned = match(near_rows)
+    device = 2 * (me // 2 ^ place // 2) + (me + place) % 2
+    touched = jnp.zeros(aligned.shape, jnp.bool_)
+    for r in range(requests):
+        for a in range(active):
+            touched = touched | ((request == r) & (device == active_ref[r, a] // per_device))
+    near = jnp.where(touched & aligned, 1.0, 0.0)
+    request, place, aligned = match(out_ref.shape[1] - near_rows)
+    far = jnp.where((request == place) & aligned, 1.0, 0.0)
+    out_ref[...] = jnp.concatenate([near, far], axis=1).astype(jnp.bfloat16)
+
+
+def finish_kernel(plan_ref, *refs):
+    part_refs, (tokens_ref, b_out_ref, out_ref) = refs[:-3], refs[-3:]
     rows, features = tokens_ref.shape
     half = features // 2
-    shape = (2 * rows, 2 * rows)
-    item, slot = iota(shape, 0), iota(shape, 1)
-    source = item % rows // nodes * SUB + item // rows * nodes + item % nodes
-    unpack = jnp.where(slot == source, 1.0, 0.0).astype(jnp.bfloat16)
-    chunk = half // len(far_refs)
+    plan = plan_ref[...]
     for j in range(0, half, WIDTH):
-        far = far_refs[j // chunk][:, j % chunk : j % chunk + WIDTH]
-        both = jnp.zeros((2 * rows, WIDTH), jnp.float32)
-        for part in (near_ref[:, j : j + WIDTH], mate_ref[:, j : j + WIDTH], far):
-            both += jnp.dot(unpack, part, preferred_element_type=jnp.float32)
+        parts = jnp.concatenate([ref[:, j : j + WIDTH] for ref in part_refs], axis=0)
+        both = jnp.dot(plan, parts, preferred_element_type=jnp.float32)
         for h in range(2):
             at = h * half + j
             mixed = (
@@ -197,7 +211,6 @@
     hbm = pl.BlockSpec(memory_space=pl.ANY)
     chips = half_count // 2
     routing = dict(chips=chips, per_device=per_device, active=active_count)
-    back_chunk = half // BACK_CHUNKS
 
     def call(kernel, shapes, in_specs, *operands, scratch=(), cost=0, limit=0):
         size = 2 * sum(rows * columns for rows, columns in shapes) + sum(x.size * 2 for x in operands)
@@ -267,31 +280,44 @@
     far_ids = other, mate_of(other)
     far_rows = to_chips(select(far_ids, far_ids, (), SELECT_COST))
     parts = call(
-        functools.partial(neuron_kernel, nodes=nodes, chips=chips, chunks=BACK_CHUNKS),
-        [(2 * SUB, half)] * chips + [(2 * SUB, back_chunk)] * (chips * BACK_CHUNKS),
+        functools.partial(neuron_kernel, nodes=nodes, chips=chips),
+        [(chips * SUB, half)] * 2 + [(2 * SUB, half)] * chips,
         [vmem] * (2 * chips + 3),
         *near_rows, *far_rows, w_in, b_in, w_out,
         scratch=[(2 * half_count * SUB, half + LANES)],
     )
-    near_parts = parts[:chips]
-    totals, far_sums = [], []
-    for c in range(BACK_CHUNKS):
-        kept, passed = gather(far_ids, parts[(1 + c) * chips : (2 + c) * chips])
-        total = kept.astype(jnp.float32) + mate_of(passed).astype(jnp.float32)
-        totals.append(total.astype(jnp.bfloat16))
-        far_sums.append(across(totals[-1]))
-    near_sent = call(
-        copy_kernel,
-        [(2 * SUB, half)] * (chips - 1),
-        [vmem] * (chips - 1) + [hbm],
-        *near_parts[1:], totals[-1],
-    )
-    near_kept, near_passed = gather(near_ids, [near_parts[0], *near_sent])
+    near_kept, near_received = parts[0], mate_of(parts[1])
+    kept, passed = gather(far_ids, parts[2:])
+    total = kept.astype(jnp.float32) + mate_of(passed).astype(jnp.float32)
+    total = total.astype(jnp.bfloat16)
+
+    def pair(places, order):
+        return call(
+            functools.partial(pair_kernel, places=places),
+            [(2 * SUB, half)] * len(places),
+            [vmem] * 2 + [hbm],
+            near_kept, near_received, order,
+        )
+
+    split = range(2, chips)
+    early = pair(split, passed)
+    far_sum = across(total)
+    late = pair(range(2), total)
+    near_back = to_chips(late + early)
+    near_count = 2 * SUB * chips
+    [plan] = call(
+        functools.partial(
+            plan_kernel, rows=rows, nodes=nodes, near_rows=near_count, per_device=per_device
+        ),
+        [(2 * rows, near_count + packed)],
+        [smem, hbm],
+        active, total,
+    )
     [mixed] = call(
-        functools.partial(finish_kernel, nodes=nodes),
+        finish_kernel,
         [(rows, features)],
-        [vmem] * (4 + BACK_CHUNKS),
-        near_kept, mate_of(near_passed), *far_sums, tokens, b_out,
+        [vmem] * (chips + 4),
+        plan, *near_back, far_sum, tokens, b_out,
     )
     return mixed
 

time: 83.9 us -> 82.6 us (0.985)
  waiting for transfers between devices: 53.3 us -> 51.3 us
    ppermute x18, waiting for transfers between devices: 53.3 us -> 51.3 us  [swap(): lax.ppermute(x, 'neuron', [(i, partner(i)) for i in range(device_count)])]
    pallas_call x8 -> x9, Pallas kernels: 7.66 us -> 7.72 us  [call(): pl.pallas_call(kernel, out_shape=[jax.ShapeDtypeStruct(shape, jnp.bfloat1...]
  transfers between devices with their start and end apart: 18 -> 18, of which waited for: 14 -> 12; matrix products, arithmetic and copies ran while one was open for 0% -> 0% of each run, Pallas kernels for 1% -> 1%
where the time goes in v4:
time: 82.6 us; the launch traced here: 82.4 us
  waiting for transfers between devices  51.3 us (62%)
  starting transfers between devices  22.1 us (27%)
  Pallas kernels  7.72 us (9%)
  local copies, waits for them, and re-layouts  1.07 us (1%)
    ppermute x18, waiting for transfers between devices, swap(): lax.ppermute(x, 'neuron', [(i, partner(i)) for i in range(device_count)])  51.3 us
    ppermute x18, starting transfers between devices, swap(): lax.ppermute(x, 'neuron', [(i, partner(i)) for i in range(device_count)])  22.1 us
    pallas_call x9, Pallas kernels, call(): pl.pallas_call(kernel, out_shape=[jax.ShapeDtypeStruct(shape, jnp.bfloat1...  7.72 us
  transfers between devices with their start and end apart: 18, of which 12 were waited for; matrix products, arithmetic and copies ran while one was open for 0% of the time, Pallas kernels for 1%

profile of v4, /device:TPU:0, one launch (start us, length us, event | category | flops | bytes accessed | tf_op | source)
XLA Modules:
  0.0 82.4 jit_solution(10831595445391812880)
XLA Ops:
  0.0 2.5 %shard_map.82.own_ids_ref.own_ref = bf16[32,6272]{1,0:T(8,128)(2,1)} custom-call(s32[4,3]{1,0:T(4,128)} %active_ref.3, bf16[16,12288]{1,0:T(8,128)(2,1)} %refs_5_.1, bf16[12288]{0:T(1024)(128)(2,1)} %gain_ref.1, bf16[12288]{0:T(1024)(128)(2,1)} %bias_ref.1), custom_call_target="tpu_custom_call" | custom-call | bytes 843800 | tf_op jit(solution)/shard_map/pallas_call | solution.py:218
  2.5 0.5 collective-permute-start.1
  2.9 3.6 %collective-permute-start = (bf16[32,6272]{1,0:T(8,128)(2,1)}, bf16[32,6272]{1,0:T(8,128)(2,1)S(1)}, u32[]{:S(2)}, u32[]{:S(2)}) collective-permute-start(bf16[32,6272]{1,0:T(8,128)(2,1)} %shard_map.82.own_ids_ref.own_ref), channel_id=1, source_target_pairs={{0,8},{1,9},{2,10},{3,11},{4,12},{5,13},{6,14},{7,15},{8,0},{9,1},... | collective-permute-start | bytes 1204232 | tf_op jit(solution)/shard_map/ppermute | solution.py:240
  6.5 1.0 %copy-done = bf16[32,6272]{1,0:T(8,128)(2,1)S(1)} copy-done((bf16[32,6272]{1,0:T(8,128)(2,1)S(1)}, bf16[32,6272]{1,0:T(8,128)(2,1)}, u32[]{:S(2)}) %copy-start) | copy-done | bytes 401432
  7.5 0.5 shard_map.83
  8.0 1.6 %collective-permute-start.2 = (bf16[16,6272]{1,0:T(8,128)(2,1)S(1)}, bf16[16,6272]{1,0:T(8,128)(2,1)S(1)}, u32[]{:S(2)}, u32[]{:S(2)}) collective-permute-start(bf16[16,6272]{1,0:T(8,128)(2,1)S(1)} %get-tuple-element.25), channel_id=1, source_target_pairs={{0,2},{1,3},{2,0},{3,1},{4,6},{5,7},{6,4},{7,5},{8,10},{9,11},{10,... | collective-permute-start | bytes 602120 | tf_op jit(solution)/shard_map/ppermute | solution.py:240
  9.6 1.6 %collective-permute-start.3 = (bf16[16,6272]{1,0:T(8,128)(2,1)S(1)}, bf16[16,6272]{1,0:T(8,128)(2,1)S(1)}, u32[]{:S(2)}, u32[]{:S(2)}) collective-permute-start(bf16[16,6272]{1,0:T(8,128)(2,1)S(1)} %get-tuple-element.26), channel_id=1, source_target_pairs={{0,4},{1,5},{2,6},{3,7},{4,0},{5,1},{6,2},{7,3},{8,12},{9,13},{10,... | collective-permute-start | bytes 602120 | tf_op jit(solution)/shard_map/ppermute | solution.py:240
  11.6 13.8 %collective-permute-done.refs_0_ = bf16[32,6272]{1,0:T(8,128)(2,1)S(1)} collective-permute-done((bf16[32,6272]{1,0:T(8,128)(2,1)}, bf16[32,6272]{1,0:T(8,128)(2,1)S(1)}, u32[]{:S(2)}, u32[]{:S(2)}) %collective-permute-start) | collective-permute-done | bytes 401440 | tf_op jit(solution)/shard_map/ppermute | solution.py:240
  25.4 2.8 %collective-permute-done.4.refs_3_ = bf16[16,6272]{1,0:T(8,128)(2,1)S(1)} collective-permute-done((bf16[16,6272]{1,0:T(8,128)(2,1)S(1)}, bf16[16,6272]{1,0:T(8,128)(2,1)S(1)}, u32[]{:S(2)}, u32[]{:S(2)}) %collective-permute-start.4) | collective-permute-done | bytes 200736 | tf_op jit(solution)/shard_map/ppermute | solution.py:240
  28.3 1.7 %collective-permute-done.5.mate_ids_ref.mate_ref = bf16[32,6272]{1,0:T(8,128)(2,1)S(1)} collective-permute-done((bf16[32,6272]{1,0:T(8,128)(2,1)S(1)}, bf16[32,6272]{1,0:T(8,128)(2,1)S(1)}, u32[]{:S(2)}, u32[]{:S(2)}) %collective-permute-start.5) | collective-permute-done | bytes 401440 | tf_op jit(solution)/shard_map/ppermute | solution.py:240
  30.1 0.5 shard_map.85
  30.6 1.5 %collective-permute-start.6 = (bf16[16,6272]{1,0:T(8,128)(2,1)S(1)}, bf16[16,6272]{1,0:T(8,128)(2,1)S(1)}, u32[]{:S(2)}, u32[]{:S(2)}) collective-permute-start(bf16[16,6272]{1,0:T(8,128)(2,1)S(1)} %get-tuple-element.30), channel_id=1, source_target_pairs={{0,2},{1,3},{2,0},{3,1},{4,6},{5,7},{6,4},{7,5},{8,10},{9,11},{10,... | collective-permute-start | bytes 602120 | tf_op jit(solution)/shard_map/ppermute | solution.py:240
  32.0 2.1 %collective-permute-start.8 = (bf16[16,6272]{1,0:T(8,128)(2,1)S(1)}, bf16[16,6272]{1,0:T(8,128)(2,1)S(1)}, u32[]{:S(2)}, u32[]{:S(2)}) collective-permute-start(bf16[16,6272]{1,0:T(8,128)(2,1)S(1)} %get-tuple-element.32), channel_id=1, source_target_pairs={{0,6},{1,7},{2,4},{3,5},{4,2},{5,3},{6,0},{7,1},{8,14},{9,15},{10,... | collective-permute-start | bytes 602120 | tf_op jit(solution)/shard_map/ppermute | solution.py:240
  34.1 3.5 %collective-permute-done.6.refs_5_ = bf16[16,6272]{1,0:T(8,128)(2,1)S(1)} collective-permute-done((bf16[16,6272]{1,0:T(8,128)(2,1)S(1)}, bf16[16,6272]{1,0:T(8,128)(2,1)S(1)}, u32[]{:S(2)}, u32[]{:S(2)}) %collective-permute-start.6) | collective-permute-done | bytes 200736 | tf_op jit(solution)/shard_map/ppermute | solution.py:240
  37.7 2.3 %collective-permute-done.7.refs_6_ = bf16[16,6272]{1,0:T(8,128)(2,1)S(1)} collective-permute-done((bf16[16,6272]{1,0:T(8,128)(2,1)S(1)}, bf16[16,6272]{1,0:T(8,128)(2,1)S(1)}, u32[]{:S(2)}, u32[]{:S(2)}) %collective-permute-start.7) | collective-permute-done | bytes 200736 | tf_op jit(solution)/shard_map/ppermute | solution.py:240
  39.9 3.2 %collective-permute-done.8.refs_7_ = bf16[16,6272]{1,0:T(8,128)(2,1)S(1)} collective-permute-done((bf16[16,6272]{1,0:T(8,128)(2,1)S(1)}, bf16[16,6272]{1,0:T(8,128)(2,1)S(1)}, u32[]{:S(2)}, u32[]{:S(2)}) %collective-permute-start.8) | collective-permute-done | bytes 200736 | tf_op jit(solution)/shard_map/ppermute | solution.py:240
  43.2 2.1 %shard_map.86 = (bf16[32,6144]{1,0:T(8,128)(2,1)S(1)}, bf16[32,6144]{1,0:T(8,128)(2,1)S(1)}, bf16[16,6144]{1,0:T(8,128)(2,1)S(1)}, bf16[16,6144]{1,0:T(8,128)(2,...) custom-call(bf16[16,6272]{1,0:T(8,128)(2,1)S(1)} %get-tuple-element.28.refs_0_, ...), custom_call_target="tpu_custom_call" | custom-call | bytes 17367552 | tf_op jit(solution)/shard_map/pallas_call | solution.py:218
  45.3 1.5 %collective-permute-start.9 = (bf16[16,6144]{1,0:T(8,128)(2,1)S(1)}, bf16[16,6144]{1,0:T(8,128)(2,1)S(1)}, u32[]{:S(2)}, u32[]{:S(2)}) collective-permute-start(bf16[16,6144]{1,0:T(8,128)(2,1)S(1)} %get-tuple-element.34), channel_id=1, source_target_pairs={{0,2},{1,3},{2,0},{3,1},{4,6},{5,7},{6,4},{7,5},{8,10},{9,11},{10,... | collective-permute-start | bytes 589832 | tf_op jit(solution)/shard_map/ppermute | solution.py:240
  47.1 1.8 %collective-permute-start.11 = (bf16[16,6144]{1,0:T(8,128)(2,1)S(1)}, bf16[16,6144]{1,0:T(8,128)(2,1)S(1)}, u32[]{:S(2)}, u32[]{:S(2)}) collective-permute-start(bf16[16,6144]{1,0:T(8,128)(2,1)S(1)} %get-tuple-element.36), channel_id=1, source_target_pairs={{0,6},{1,7},{2,4},{3,5},{4,2},{5,3},{6,0},{7,1},{8,14},{9,15},{10,... | collective-permute-start | bytes 589832 | tf_op jit(solution)/shard_map/ppermute | solution.py:240
  48.9 3.4 %collective-permute-done.9.refs_1_ = bf16[16,6144]{1,0:T(8,128)(2,1)S(1)} collective-permute-done((bf16[16,6144]{1,0:T(8,128)(2,1)S(1)}, bf16[16,6144]{1,0:T(8,128)(2,1)S(1)}, u32[]{:S(2)}, u32[]{:S(2)}) %collective-permute-start.9) | collective-permute-done | bytes 196640 | tf_op jit(solution)/shard_map/ppermute | solution.py:240
  52.3 2.1 %collective-permute-done.10.refs_2_ = bf16[16,6144]{1,0:T(8,128)(2,1)S(1)} collective-permute-done((bf16[16,6144]{1,0:T(8,128)(2,1)S(1)}, bf16[16,6144]{1,0:T(8,128)(2,1)S(1)}, u32[]{:S(2)}, u32[]{:S(2)}) %collective-permute-start.10) | collective-permute-done | bytes 196640 | tf_op jit(solution)/shard_map/ppermute | solution.py:240
  54.4 2.1 %collective-permute-done.11.refs_3_ = bf16[16,6144]{1,0:T(8,128)(2,1)S(1)} collective-permute-done((bf16[16,6144]{1,0:T(8,128)(2,1)S(1)}, bf16[16,6144]{1,0:T(8,128)(2,1)S(1)}, u32[]{:S(2)}, u32[]{:S(2)}) %collective-permute-start.11) | collective-permute-done | bytes 196640 | tf_op jit(solution)/shard_map/ppermute | solution.py:240
  57.0 0.5 collective-permute-start.13
  57.5 1.2 %collective-permute-done.12 = bf16[32,6144]{1,0:T(8,128)(2,1)S(1)} collective-permute-done((bf16[32,6144]{1,0:T(8,128)(2,1)S(1)}, bf16[32,6144]{1,0:T(8,128)(2,1)S(1)}, u32[]{:S(2)}, u32[]{:S(2)}) %collective-permute-start.12) | collective-permute-done | bytes 393248 | tf_op jit(solution)/shard_map/ppermute | solution.py:240
  58.9 3.1 %collective-permute-start.17 = (bf16[32,6144]{1,0:T(8,128)(2,1)S(1)}, bf16[32,6144]{1,0:T(8,128)(2,1)S(1)}, u32[]{:S(2)}, u32[]{:S(2)}) collective-permute-start(bf16[32,6144]{1,0:T(8,128)(2,1)S(1)} %add_convert_fusion.order_ref.refs_0_), channel_id=1, source_target_pairs={{0,8},{1,9},{2,10},{3,11},{4,12},{5,13},{6,14},{7,15},{8,0},{9,1},... | collective-permute-start | bytes 1179656 | tf_op jit(solution)/shard_map/ppermute | solution.py:240
  62.0 1.5 %collective-permute-start.15 = (bf16[16,6144]{1,0:T(8,128)(2,1)S(1)}, bf16[16,6144]{1,0:T(8,128)(2,1)S(1)}, u32[]{:S(2)}, u32[]{:S(2)}) collective-permute-start(bf16[16,6144]{1,0:T(8,128)(2,1)S(1)} %get-tuple-element.43), channel_id=1, source_target_pairs={{0,4},{1,5},{2,6},{3,7},{4,0},{5,1},{6,2},{7,3},{8,12},{9,13},{10,... | collective-permute-start | bytes 589832 | tf_op jit(solution)/shard_map/ppermute | solution.py:240
  63.5 1.5 %collective-permute-start.16 = (bf16[16,6144]{1,0:T(8,128)(2,1)S(1)}, bf16[16,6144]{1,0:T(8,128)(2,1)S(1)}, u32[]{:S(2)}, u32[]{:S(2)}) collective-permute-start(bf16[16,6144]{1,0:T(8,128)(2,1)S(1)} %get-tuple-element.44), channel_id=1, source_target_pairs={{0,6},{1,7},{2,4},{3,5},{4,2},{5,3},{6,0},{7,1},{8,14},{9,15},{10,... | collective-permute-start | bytes 589832 | tf_op jit(solution)/shard_map/ppermute | solution.py:240
  65.0 0.7 collective-permute-start.14
  65.7 0.6 shard_map.88.plan_ref
  66.3 9.4 %collective-permute-done.15.refs_2_ = bf16[16,6144]{1,0:T(8,128)(2,1)S(1)} collective-permute-done((bf16[16,6144]{1,0:T(8,128)(2,1)S(1)}, bf16[16,6144]{1,0:T(8,128)(2,1)S(1)}, u32[]{:S(2)}, u32[]{:S(2)}) %collective-permute-start.15) | collective-permute-done | bytes 196640 | tf_op jit(solution)/shard_map/ppermute | solution.py:240
  75.7 5.6 %collective-permute-done.16.refs_3_ = bf16[16,6144]{1,0:T(8,128)(2,1)S(1)} collective-permute-done((bf16[16,6144]{1,0:T(8,128)(2,1)S(1)}, bf16[16,6144]{1,0:T(8,128)(2,1)S(1)}, u32[]{:S(2)}, u32[]{:S(2)}) %collective-permute-start.16) | collective-permute-done | bytes 196640 | tf_op jit(solution)/shard_map/ppermute | solution.py:240
  81.3 1.1 %shard_map.91 = bf16[16,12288]{1,0:T(8,128)(2,1)} custom-call(bf16[32,96]{1,0:T(8,128)(2,1)S(1)} %shard_map.88.plan_ref, bf16[16,6144]{1,0:T(8,128)(2,1)S(1)} %get-tuple-element.41.refs_0_, bf16[16,6144]{1,0:T(8,128)(2,1)S(1)} %collective-permute-done.14.refs_1_, bf16[16,6144]{1,0:T(8,128)(2,1)S(1)} %collective-permute-done.15.refs_2_, ...), custom_call_target="tpu_custom_call" | custom-call | bytes 1996800 | tf_op jit(solution)/shard_map/pallas_call | solution.py:218
  (35 shorter events, 1.5 us)
Async XLA Ops:
  2.5 4.0 %collective-permute-start.1 = (bf16[32,6272]{1,0:T(8,128)(2,1)}, bf16[32,6272]{1,0:T(8,128)(2,1)S(1)}, u32[]{:S(2)}, u32[]{:S(2)}) collective-permute-start(bf16[32,6272]{1,0:T(8,128)(2,1)} %shard_map.82.own_ids_ref.own_ref), channel_id=1, source_target_pairs={{0,1},{1,0},{2,3},{3,2},{4,5},{5,4},{6,7},{7,6},{8,9},{9,8},{10,11... | collective-permute-start | bytes 1204232 | tf_op jit(solution)/shard_map/ppermute | solution.py:240
  2.9 22.5 %collective-permute-start = (bf16[32,6272]{1,0:T(8,128)(2,1)}, bf16[32,6272]{1,0:T(8,128)(2,1)S(1)}, u32[]{:S(2)}, u32[]{:S(2)}) collective-permute-start(bf16[32,6272]{1,0:T(8,128)(2,1)} %shard_map.82.own_ids_ref.own_ref), channel_id=1, source_target_pairs={{0,8},{1,9},{2,10},{3,11},{4,12},{5,13},{6,14},{7,15},{8,0},{9,1},... | collective-permute-start | bytes 1204232 | tf_op jit(solution)/shard_map/ppermute | solution.py:240
  6.5 1.0 %copy-start = (bf16[32,6272]{1,0:T(8,128)(2,1)S(1)}, bf16[32,6272]{1,0:T(8,128)(2,1)}, u32[]{:S(2)}) copy-start(bf16[32,6272]{1,0:T(8,128)(2,1)} %shard_map.82.own_ids_ref.own_ref) | copy-start | bytes 1204228
  8.0 17.3 %collective-permute-start.2 = (bf16[16,6272]{1,0:T(8,128)(2,1)S(1)}, bf16[16,6272]{1,0:T(8,128)(2,1)S(1)}, u32[]{:S(2)}, u32[]{:S(2)}) collective-permute-start(bf16[16,6272]{1,0:T(8,128)(2,1)S(1)} %get-tuple-element.25), channel_id=1, source_target_pairs={{0,2},{1,3},{2,0},{3,1},{4,6},{5,7},{6,4},{7,5},{8,10},{9,11},{10,... | collective-permute-start | bytes 602120 | tf_op jit(solution)/shard_map/ppermute | solution.py:240
  9.6 15.8 %collective-permute-start.3 = (bf16[16,6272]{1,0:T(8,128)(2,1)S(1)}, bf16[16,6272]{1,0:T(8,128)(2,1)S(1)}, u32[]{:S(2)}, u32[]{:S(2)}) collective-permute-start(bf16[16,6272]{1,0:T(8,128)(2,1)S(1)} %get-tuple-element.26), channel_id=1, source_target_pairs={{0,4},{1,5},{2,6},{3,7},{4,0},{5,1},{6,2},{7,3},{8,12},{9,13},{10,... | collective-permute-start | bytes 602120 | tf_op jit(solution)/shard_map/ppermute | solution.py:240
  11.2 17.1 %collective-permute-start.4 = (bf16[16,6272]{1,0:T(8,128)(2,1)S(1)}, bf16[16,6272]{1,0:T(8,128)(2,1)S(1)}, u32[]{:S(2)}, u32[]{:S(2)}) collective-permute-start(bf16[16,6272]{1,0:T(8,128)(2,1)S(1)} %get-tuple-element.27), channel_id=1, source_target_pairs={{0,6},{1,7},{2,4},{3,5},{4,2},{5,3},{6,0},{7,1},{8,14},{9,15},{10,... | collective-permute-start | bytes 602120 | tf_op jit(solution)/shard_map/ppermute | solution.py:240
  28.2 14.9 %slice-start = ((s8[6291456]{0:T(1024)(128)(4,1)}), s8[4194304]{0:T(1024)(128)(4,1)S(1)}, s32[]{:S(2)}) async-start(s8[6291456]{0:T(1024)(128)(4,1)} %bitcast), calls=%async_computation | async-start | bytes 8388608
  28.2 14.9 %slice-start.2 = ((s8[6291456]{0:T(1024)(128)(4,1)}), s8[4194304]{0:T(1024)(128)(4,1)S(1)}, s32[]{:S(2)}) async-start(s8[6291456]{0:T(1024)(128)(4,1)} %bitcast.2), calls=%async_computation.2 | async-start | bytes 8388608
  28.2 14.9 %slice-start.1 = ((s8[6291456]{0:T(1024)(128)(4,1)}), s8[2097152]{0:T(1024)(128)(4,1)S(1)}, s32[]{:S(2)}) async-start(s8[6291456]{0:T(1024)(128)(4,1)} %bitcast), calls=%async_computation.1 | async-start | bytes 4194304
  28.2 14.9 %slice-start.3 = ((s8[6291456]{0:T(1024)(128)(4,1)}), s8[2097152]{0:T(1024)(128)(4,1)S(1)}, s32[]{:S(2)}) async-start(s8[6291456]{0:T(1024)(128)(4,1)} %bitcast.2), calls=%async_computation.3 | async-start | bytes 4194304
  28.2 14.9 %copy-start.4 = (bf16[256]{0:T(256)(128)(2,1)S(1)}, bf16[256]{0:T(256)(128)(2,1)}, u32[]{:S(2)}) copy-start(bf16[256]{0:T(256)(128)(2,1)} %refs_9_.1) | copy-start | bytes 1540
  28.3 1.8 %collective-permute-start.5 = (bf16[32,6272]{1,0:T(8,128)(2,1)S(1)}, bf16[32,6272]{1,0:T(8,128)(2,1)S(1)}, u32[]{:S(2)}, u32[]{:S(2)}) collective-permute-start(bf16[32,6272]{1,0:T(8,128)(2,1)S(1)} %shard_map.84.own_ids_ref.own_ref), channel_id=1, source_target_pairs={{0,1},{1,0},{2,3},{3,2},{4,5},{5,4},{6,7},{7,6},{8,9},{9,8},{10,11... | collective-permute-start | bytes 1204232 | tf_op jit(solution)/shard_map/ppermute | solution.py:240
  30.6 7.1 %collective-permute-start.6 = (bf16[16,6272]{1,0:T(8,128)(2,1)S(1)}, bf16[16,6272]{1,0:T(8,128)(2,1)S(1)}, u32[]{:S(2)}, u32[]{:S(2)}) collective-permute-start(bf16[16,6272]{1,0:T(8,128)(2,1)S(1)} %get-tuple-element.30), channel_id=1, source_target_pairs={{0,2},{1,3},{2,0},{3,1},{4,6},{5,7},{6,4},{7,5},{8,10},{9,11},{10,... | collective-permute-start | bytes 602120 | tf_op jit(solution)/shard_map/ppermute | solution.py:240
  32.0 7.9 %collective-permute-start.7 = (bf16[16,6272]{1,0:T(8,128)(2,1)S(1)}, bf16[16,6272]{1,0:T(8,128)(2,1)S(1)}, u32[]{:S(2)}, u32[]{:S(2)}) collective-permute-start(bf16[16,6272]{1,0:T(8,128)(2,1)S(1)} %get-tuple-element.31), channel_id=1, source_target_pairs={{0,4},{1,5},{2,6},{3,7},{4,0},{5,1},{6,2},{7,3},{8,12},{9,13},{10,... | collective-permute-start | bytes 602120 | tf_op jit(solution)/shard_map/ppermute | solution.py:240
  32.0 11.1 %collective-permute-start.8 = (bf16[16,6272]{1,0:T(8,128)(2,1)S(1)}, bf16[16,6272]{1,0:T(8,128)(2,1)S(1)}, u32[]{:S(2)}, u32[]{:S(2)}) collective-permute-start(bf16[16,6272]{1,0:T(8,128)(2,1)S(1)} %get-tuple-element.32), channel_id=1, source_target_pairs={{0,6},{1,7},{2,4},{3,5},{4,2},{5,3},{6,0},{7,1},{8,14},{9,15},{10,... | collective-permute-start | bytes 602120 | tf_op jit(solution)/shard_map/ppermute | solution.py:240
  43.2 22.5 %copy-start.3 = (s32[4,3]{1,0:T(4,128)S(1)}, s32[4,3]{1,0:T(4,128)}, u32[]{:S(2)}) copy-start(s32[4,3]{1,0:T(4,128)} %active_ref.3) | copy-start | bytes 148
  43.2 38.1 %copy-start.1 = (bf16[16,12288]{1,0:T(8,128)(2,1)S(1)}, bf16[16,12288]{1,0:T(8,128)(2,1)}, u32[]{:S(2)}) copy-start(bf16[16,12288]{1,0:T(8,128)(2,1)} %refs_5_.1) | copy-start | bytes 1179652
  43.2 38.1 %copy-start.2 = (bf16[12288]{0:T(1024)(128)(2,1)S(1)}, bf16[12288]{0:T(1024)(128)(2,1)}, u32[]{:S(2)}) copy-start(bf16[12288]{0:T(1024)(128)(2,1)} %refs_6_.1) | copy-start | bytes 73732
  45.3 7.0 %collective-permute-start.9 = (bf16[16,6144]{1,0:T(8,128)(2,1)S(1)}, bf16[16,6144]{1,0:T(8,128)(2,1)S(1)}, u32[]{:S(2)}, u32[]{:S(2)}) collective-permute-start(bf16[16,6144]{1,0:T(8,128)(2,1)S(1)} %get-tuple-element.34), channel_id=1, source_target_pairs={{0,2},{1,3},{2,0},{3,1},{4,6},{5,7},{6,4},{7,5},{8,10},{9,11},{10,... | collective-permute-start | bytes 589832 | tf_op jit(solution)/shard_map/ppermute | solution.py:240
  46.8 7.6 %collective-permute-start.10 = (bf16[16,6144]{1,0:T(8,128)(2,1)S(1)}, bf16[16,6144]{1,0:T(8,128)(2,1)S(1)}, u32[]{:S(2)}, u32[]{:S(2)}) collective-permute-start(bf16[16,6144]{1,0:T(8,128)(2,1)S(1)} %get-tuple-element.35), channel_id=1, source_target_pairs={{0,4},{1,5},{2,6},{3,7},{4,0},{5,1},{6,2},{7,3},{8,12},{9,13},{10,... | collective-permute-start | bytes 589832 | tf_op jit(solution)/shard_map/ppermute | solution.py:240
  47.1 9.5 %collective-permute-start.11 = (bf16[16,6144]{1,0:T(8,128)(2,1)S(1)}, bf16[16,6144]{1,0:T(8,128)(2,1)S(1)}, u32[]{:S(2)}, u32[]{:S(2)}) collective-permute-start(bf16[16,6144]{1,0:T(8,128)(2,1)S(1)} %get-tuple-element.36), channel_id=1, source_target_pairs={{0,6},{1,7},{2,4},{3,5},{4,2},{5,3},{6,0},{7,1},{8,14},{9,15},{10,... | collective-permute-start | bytes 589832 | tf_op jit(solution)/shard_map/ppermute | solution.py:240
  57.0 1.8 %collective-permute-start.12 = (bf16[32,6144]{1,0:T(8,128)(2,1)S(1)}, bf16[32,6144]{1,0:T(8,128)(2,1)S(1)}, u32[]{:S(2)}, u32[]{:S(2)}) collective-permute-start(bf16[32,6144]{1,0:T(8,128)(2,1)S(1)} %get-tuple-element.38.refs_0_), channel_id=1, source_target_pairs={{0,1},{1,0},{2,3},{3,2},{4,5},{5,4},{6,7},{7,6},{8,9},{9,8},{10,11... | collective-permute-start | bytes 1179656 | tf_op jit(solution)/shard_map/ppermute | solution.py:240
  57.0 4.9 %collective-permute-start.13 = (bf16[32,6144]{1,0:T(8,128)(2,1)S(1)}, bf16[32,6144]{1,0:T(8,128)(2,1)S(1)}, u32[]{:S(2)}, u32[]{:S(2)}) collective-permute-start(bf16[32,6144]{1,0:T(8,128)(2,1)S(1)} %get-tuple-element.40), channel_id=1, source_target_pairs={{0,1},{1,0},{2,3},{3,2},{4,5},{5,4},{6,7},{7,6},{8,9},{9,8},{10,11... | collective-permute-start | bytes 1179656 | tf_op jit(solution)/shard_map/ppermute | solution.py:240
  58.9 22.5 %collective-permute-start.17 = (bf16[32,6144]{1,0:T(8,128)(2,1)S(1)}, bf16[32,6144]{1,0:T(8,128)(2,1)S(1)}, u32[]{:S(2)}, u32[]{:S(2)}) collective-permute-start(bf16[32,6144]{1,0:T(8,128)(2,1)S(1)} %add_convert_fusion.order_ref.refs_0_), channel_id=1, source_target_pairs={{0,8},{1,9},{2,10},{3,11},{4,12},{5,13},{6,14},{7,15},{8,0},{9,1},... | collective-permute-start | bytes 1179656 | tf_op jit(solution)/shard_map/ppermute | solution.py:240
  62.0 13.7 %collective-permute-start.15 = (bf16[16,6144]{1,0:T(8,128)(2,1)S(1)}, bf16[16,6144]{1,0:T(8,128)(2,1)S(1)}, u32[]{:S(2)}, u32[]{:S(2)}) collective-permute-start(bf16[16,6144]{1,0:T(8,128)(2,1)S(1)} %get-tuple-element.43), channel_id=1, source_target_pairs={{0,4},{1,5},{2,6},{3,7},{4,0},{5,1},{6,2},{7,3},{8,12},{9,13},{10,... | collective-permute-start | bytes 589832 | tf_op jit(solution)/shard_map/ppermute | solution.py:240
  63.5 17.8 %collective-permute-start.16 = (bf16[16,6144]{1,0:T(8,128)(2,1)S(1)}, bf16[16,6144]{1,0:T(8,128)(2,1)S(1)}, u32[]{:S(2)}, u32[]{:S(2)}) collective-permute-start(bf16[16,6144]{1,0:T(8,128)(2,1)S(1)} %get-tuple-element.44), channel_id=1, source_target_pairs={{0,6},{1,7},{2,4},{3,5},{4,2},{5,3},{6,0},{7,1},{8,14},{9,15},{10,... | collective-permute-start | bytes 589832 | tf_op jit(solution)/shard_map/ppermute | solution.py:240
  65.0 16.3 %collective-permute-start.14 = (bf16[16,6144]{1,0:T(8,128)(2,1)S(1)}, bf16[16,6144]{1,0:T(8,128)(2,1)S(1)}, u32[]{:S(2)}, u32[]{:S(2)}) collective-permute-start(bf16[16,6144]{1,0:T(8,128)(2,1)S(1)} %get-tuple-element.42), channel_id=1, source_target_pairs={{0,2},{1,3},{2,0},{3,1},{4,6},{5,7},{6,4},{7,5},{8,10},{9,11},{10,... | collective-permute-start | bytes 589832 | tf_op jit(solution)/shard_map/ppermute | solution.py:240

commit v5 on v4

--- a/solution.py
+++ b/solution.py
@@ -42,13 +42,13 @@
     half = features // 2
     packed = 2 * rows
     requests, active = active_ref.shape
-    total = jnp.zeros((rows, LANES), jnp.float32)
-    for j in range(0, features, LANES):
-        total += tokens_ref[:, j : j + LANES].astype(jnp.float32)
+    total = jnp.zeros((rows, WIDTH), jnp.float32)
+    for j in range(0, features, WIDTH):
+        total += tokens_ref[:, j : j + WIDTH].astype(jnp.float32)
     mean = jnp.sum(total, axis=1, keepdims=True) / features
-    total = jnp.zeros((rows, LANES), jnp.float32)
-    for j in range(0, features, LANES):
-        centred = tokens_ref[:, j : j + LANES].astype(jnp.float32) - mean
+    total = jnp.zeros((rows, WIDTH), jnp.float32)
+    for j in range(0, features, WIDTH):
+        centred = tokens_ref[:, j : j + WIDTH].astype(jnp.float32) - mean
         total += centred * centred
     scale = lax.rsqrt(jnp.sum(total, axis=1, keepdims=True) / features + epsilon)
     shape = (packed, packed)
@@ -301,6 +301,7 @@
 
     split = range(2, chips)
     early = pair(split, passed)
+    total = after(total, *early)
     far_sum = across(total)
     late = pair(range(2), total)
     near_back = to_chips(late + early)

time: 82.6 us -> 82.4 us (level)
  transfers between devices with their start and end apart: 18 -> 18, of which waited for: 12 -> 12; matrix products, arithmetic and copies ran while one was open for 0% -> 0% of each run, Pallas kernels for 1% -> 2%
where the time goes in v5:
time: 82.4 us; the launch traced here: 82.3 us
  waiting for transfers between devices  51.8 us (63%)
  starting transfers between devices  21.5 us (26%)
  Pallas kernels  7.62 us (9%)
  local copies, waits for them, and re-layouts  1.07 us (1%)
    ppermute x18, waiting for transfers between devices, swap(): lax.ppermute(x, 'neuron', [(i, partner(i)) for i in range(device_count)])  51.8 us
    ppermute x18, starting transfers between devices, swap(): lax.ppermute(x, 'neuron', [(i, partner(i)) for i in range(device_count)])  21.5 us
    pallas_call x9, Pallas kernels, call(): pl.pallas_call(kernel, out_shape=[jax.ShapeDtypeStruct(shape, jnp.bfloat1...  7.62 us
  transfers between devices with their start and end apart: 18, of which 12 were waited for; matrix products, arithmetic and copies ran while one was open for 0% of the time, Pallas kernels for 2%

profile of v5, /device:TPU:0, one launch (start us, length us, event | category | flops | bytes accessed | tf_op | source)
XLA Modules:
  0.0 82.3 jit_solution(14986924571826014245)
XLA Ops:
  0.0 2.4 %shard_map.82.own_ids_ref.own_ref = bf16[32,6272]{1,0:T(8,128)(2,1)} custom-call(s32[4,3]{1,0:T(4,128)} %active_ref.3, bf16[16,12288]{1,0:T(8,128)(2,1)} %refs_5_.1, bf16[12288]{0:T(1024)(128)(2,1)} %gain_ref.1, bf16[12288]{0:T(1024)(128)(2,1)} %bias_ref.1), custom_call_target="tpu_custom_call" | custom-call | bytes 843800 | tf_op jit(solution)/shard_map/pallas_call | solution.py:218
  2.4 0.5 collective-permute-start.1
  2.8 3.6 %collective-permute-start = (bf16[32,6272]{1,0:T(8,128)(2,1)}, bf16[32,6272]{1,0:T(8,128)(2,1)S(1)}, u32[]{:S(2)}, u32[]{:S(2)}) collective-permute-start(bf16[32,6272]{1,0:T(8,128)(2,1)} %shard_map.82.own_ids_ref.own_ref), channel_id=1, source_target_pairs={{0,8},{1,9},{2,10},{3,11},{4,12},{5,13},{6,14},{7,15},{8,0},{9,1},... | collective-permute-start | bytes 1204232 | tf_op jit(solution)/shard_map/ppermute | solution.py:240
  6.4 1.0 %copy-done = bf16[32,6272]{1,0:T(8,128)(2,1)S(1)} copy-done((bf16[32,6272]{1,0:T(8,128)(2,1)S(1)}, bf16[32,6272]{1,0:T(8,128)(2,1)}, u32[]{:S(2)}) %copy-start) | copy-done | bytes 401432
  7.4 0.5 shard_map.83
  7.9 1.6 %collective-permute-start.2 = (bf16[16,6272]{1,0:T(8,128)(2,1)S(1)}, bf16[16,6272]{1,0:T(8,128)(2,1)S(1)}, u32[]{:S(2)}, u32[]{:S(2)}) collective-permute-start(bf16[16,6272]{1,0:T(8,128)(2,1)S(1)} %get-tuple-element.25), channel_id=1, source_target_pairs={{0,2},{1,3},{2,0},{3,1},{4,6},{5,7},{6,4},{7,5},{8,10},{9,11},{10,... | collective-permute-start | bytes 602120 | tf_op jit(solution)/shard_map/ppermute | solution.py:240
  9.5 1.6 %collective-permute-start.3 = (bf16[16,6272]{1,0:T(8,128)(2,1)S(1)}, bf16[16,6272]{1,0:T(8,128)(2,1)S(1)}, u32[]{:S(2)}, u32[]{:S(2)}) collective-permute-start(bf16[16,6272]{1,0:T(8,128)(2,1)S(1)} %get-tuple-element.26), channel_id=1, source_target_pairs={{0,4},{1,5},{2,6},{3,7},{4,0},{5,1},{6,2},{7,3},{8,12},{9,13},{10,... | collective-permute-start | bytes 602120 | tf_op jit(solution)/shard_map/ppermute | solution.py:240
  11.1 0.4 collective-permute-start.4
  11.5 13.8 %collective-permute-done.refs_0_ = bf16[32,6272]{1,0:T(8,128)(2,1)S(1)} collective-permute-done((bf16[32,6272]{1,0:T(8,128)(2,1)}, bf16[32,6272]{1,0:T(8,128)(2,1)S(1)}, u32[]{:S(2)}, u32[]{:S(2)}) %collective-permute-start) | collective-permute-done | bytes 401440 | tf_op jit(solution)/shard_map/ppermute | solution.py:240
  25.3 2.8 %collective-permute-done.4.refs_3_ = bf16[16,6272]{1,0:T(8,128)(2,1)S(1)} collective-permute-done((bf16[16,6272]{1,0:T(8,128)(2,1)S(1)}, bf16[16,6272]{1,0:T(8,128)(2,1)S(1)}, u32[]{:S(2)}, u32[]{:S(2)}) %collective-permute-start.4) | collective-permute-done | bytes 200736 | tf_op jit(solution)/shard_map/ppermute | solution.py:240
  28.2 1.7 %collective-permute-done.5.mate_ids_ref.mate_ref = bf16[32,6272]{1,0:T(8,128)(2,1)S(1)} collective-permute-done((bf16[32,6272]{1,0:T(8,128)(2,1)S(1)}, bf16[32,6272]{1,0:T(8,128)(2,1)S(1)}, u32[]{:S(2)}, u32[]{:S(2)}) %collective-permute-start.5) | collective-permute-done | bytes 401440 | tf_op jit(solution)/shard_map/ppermute | solution.py:240
  29.9 0.5 shard_map.85
  30.4 1.5 %collective-permute-start.6 = (bf16[16,6272]{1,0:T(8,128)(2,1)S(1)}, bf16[16,6272]{1,0:T(8,128)(2,1)S(1)}, u32[]{:S(2)}, u32[]{:S(2)}) collective-permute-start(bf16[16,6272]{1,0:T(8,128)(2,1)S(1)} %get-tuple-element.30), channel_id=1, source_target_pairs={{0,2},{1,3},{2,0},{3,1},{4,6},{5,7},{6,4},{7,5},{8,10},{9,11},{10,... | collective-permute-start | bytes 602120 | tf_op jit(solution)/shard_map/ppermute | solution.py:240
  32.0 2.0 %collective-permute-start.8 = (bf16[16,6272]{1,0:T(8,128)(2,1)S(1)}, bf16[16,6272]{1,0:T(8,128)(2,1)S(1)}, u32[]{:S(2)}, u32[]{:S(2)}) collective-permute-start(bf16[16,6272]{1,0:T(8,128)(2,1)S(1)} %get-tuple-element.32), channel_id=1, source_target_pairs={{0,6},{1,7},{2,4},{3,5},{4,2},{5,3},{6,0},{7,1},{8,14},{9,15},{10,... | collective-permute-start | bytes 602120 | tf_op jit(solution)/shard_map/ppermute | solution.py:240
  34.0 3.5 %collective-permute-done.6.refs_5_ = bf16[16,6272]{1,0:T(8,128)(2,1)S(1)} collective-permute-done((bf16[16,6272]{1,0:T(8,128)(2,1)S(1)}, bf16[16,6272]{1,0:T(8,128)(2,1)S(1)}, u32[]{:S(2)}, u32[]{:S(2)}) %collective-permute-start.6) | collective-permute-done | bytes 200736 | tf_op jit(solution)/shard_map/ppermute | solution.py:240
  37.5 2.3 %collective-permute-done.7.refs_6_ = bf16[16,6272]{1,0:T(8,128)(2,1)S(1)} collective-permute-done((bf16[16,6272]{1,0:T(8,128)(2,1)S(1)}, bf16[16,6272]{1,0:T(8,128)(2,1)S(1)}, u32[]{:S(2)}, u32[]{:S(2)}) %collective-permute-start.7) | collective-permute-done | bytes 200736 | tf_op jit(solution)/shard_map/ppermute | solution.py:240
  39.8 3.2 %collective-permute-done.8.refs_7_ = bf16[16,6272]{1,0:T(8,128)(2,1)S(1)} collective-permute-done((bf16[16,6272]{1,0:T(8,128)(2,1)S(1)}, bf16[16,6272]{1,0:T(8,128)(2,1)S(1)}, u32[]{:S(2)}, u32[]{:S(2)}) %collective-permute-start.8) | collective-permute-done | bytes 200736 | tf_op jit(solution)/shard_map/ppermute | solution.py:240
  43.1 2.1 %shard_map.86 = (bf16[32,6144]{1,0:T(8,128)(2,1)S(1)}, bf16[32,6144]{1,0:T(8,128)(2,1)S(1)}, bf16[16,6144]{1,0:T(8,128)(2,1)S(1)}, bf16[16,6144]{1,0:T(8,128)(2,...) custom-call(bf16[16,6272]{1,0:T(8,128)(2,1)S(1)} %get-tuple-element.28.refs_0_, ...), custom_call_target="tpu_custom_call" | custom-call | bytes 17367552 | tf_op jit(solution)/shard_map/pallas_call | solution.py:218
  45.2 1.5 %collective-permute-start.9 = (bf16[16,6144]{1,0:T(8,128)(2,1)S(1)}, bf16[16,6144]{1,0:T(8,128)(2,1)S(1)}, u32[]{:S(2)}, u32[]{:S(2)}) collective-permute-start(bf16[16,6144]{1,0:T(8,128)(2,1)S(1)} %get-tuple-element.34), channel_id=1, source_target_pairs={{0,2},{1,3},{2,0},{3,1},{4,6},{5,7},{6,4},{7,5},{8,10},{9,11},{10,... | collective-permute-start | bytes 589832 | tf_op jit(solution)/shard_map/ppermute | solution.py:240
  47.0 1.7 %collective-permute-start.11 = (bf16[16,6144]{1,0:T(8,128)(2,1)S(1)}, bf16[16,6144]{1,0:T(8,128)(2,1)S(1)}, u32[]{:S(2)}, u32[]{:S(2)}) collective-permute-start(bf16[16,6144]{1,0:T(8,128)(2,1)S(1)} %get-tuple-element.36), channel_id=1, source_target_pairs={{0,6},{1,7},{2,4},{3,5},{4,2},{5,3},{6,0},{7,1},{8,14},{9,15},{10,... | collective-permute-start | bytes 589832 | tf_op jit(solution)/shard_map/ppermute | solution.py:240
  48.7 3.4 %collective-permute-done.9.refs_1_ = bf16[16,6144]{1,0:T(8,128)(2,1)S(1)} collective-permute-done((bf16[16,6144]{1,0:T(8,128)(2,1)S(1)}, bf16[16,6144]{1,0:T(8,128)(2,1)S(1)}, u32[]{:S(2)}, u32[]{:S(2)}) %collective-permute-start.9) | collective-permute-done | bytes 196640 | tf_op jit(solution)/shard_map/ppermute | solution.py:240
  52.2 2.1 %collective-permute-done.10.refs_2_ = bf16[16,6144]{1,0:T(8,128)(2,1)S(1)} collective-permute-done((bf16[16,6144]{1,0:T(8,128)(2,1)S(1)}, bf16[16,6144]{1,0:T(8,128)(2,1)S(1)}, u32[]{:S(2)}, u32[]{:S(2)}) %collective-permute-start.10) | collective-permute-done | bytes 196640 | tf_op jit(solution)/shard_map/ppermute | solution.py:240
  54.3 2.1 %collective-permute-done.11.refs_3_ = bf16[16,6144]{1,0:T(8,128)(2,1)S(1)} collective-permute-done((bf16[16,6144]{1,0:T(8,128)(2,1)S(1)}, bf16[16,6144]{1,0:T(8,128)(2,1)S(1)}, u32[]{:S(2)}, u32[]{:S(2)}) %collective-permute-start.11) | collective-permute-done | bytes 196640 | tf_op jit(solution)/shard_map/ppermute | solution.py:240
  57.0 1.7 %collective-permute-done.12 = bf16[32,6144]{1,0:T(8,128)(2,1)S(1)} collective-permute-done((bf16[32,6144]{1,0:T(8,128)(2,1)S(1)}, bf16[32,6144]{1,0:T(8,128)(2,1)S(1)}, u32[]{:S(2)}, u32[]{:S(2)}) %collective-permute-start.12) | collective-permute-done | bytes 393248 | tf_op jit(solution)/shard_map/ppermute | solution.py:240
  58.8 3.1 %collective-permute-start.17 = (bf16[32,6144]{1,0:T(8,128)(2,1)S(1)}, bf16[32,6144]{1,0:T(8,128)(2,1)S(1)}, u32[]{:S(2)}, u32[]{:S(2)}) collective-permute-start(bf16[32,6144]{1,0:T(8,128)(2,1)S(1)} %shard_map.89.order_ref.refs_0_), channel_id=1, source_target_pairs={{0,8},{1,9},{2,10},{3,11},{4,12},{5,13},{6,14},{7,15},{8,0},{9,1},... | collective-permute-start | bytes 1179656 | tf_op jit(solution)/shard_map/ppermute | solution.py:240
  61.8 1.4 %collective-permute-start.15 = (bf16[16,6144]{1,0:T(8,128)(2,1)S(1)}, bf16[16,6144]{1,0:T(8,128)(2,1)S(1)}, u32[]{:S(2)}, u32[]{:S(2)}) collective-permute-start(bf16[16,6144]{1,0:T(8,128)(2,1)S(1)} %get-tuple-element.41.refs_1_), channel_id=1, source_target_pairs={{0,4},{1,5},{2,6},{3,7},{4,0},{5,1},{6,2},{7,3},{8,12},{9,13},{10,... | collective-permute-start | bytes 589832 | tf_op jit(solution)/shard_map/ppermute | solution.py:240
  63.2 1.6 %collective-permute-start.16 = (bf16[16,6144]{1,0:T(8,128)(2,1)S(1)}, bf16[16,6144]{1,0:T(8,128)(2,1)S(1)}, u32[]{:S(2)}, u32[]{:S(2)}) collective-permute-start(bf16[16,6144]{1,0:T(8,128)(2,1)S(1)} %get-tuple-element.42.refs_2_), channel_id=1, source_target_pairs={{0,6},{1,7},{2,4},{3,5},{4,2},{5,3},{6,0},{7,1},{8,14},{9,15},{10,... | collective-permute-start | bytes 589832 | tf_op jit(solution)/shard_map/ppermute | solution.py:240
  64.8 0.6 collective-permute-start.14
  65.4 0.6 shard_map.90.plan_ref
  66.1 9.5 %collective-permute-done.15.refs_2_ = bf16[16,6144]{1,0:T(8,128)(2,1)S(1)} collective-permute-done((bf16[16,6144]{1,0:T(8,128)(2,1)S(1)}, bf16[16,6144]{1,0:T(8,128)(2,1)S(1)}, u32[]{:S(2)}, u32[]{:S(2)}) %collective-permute-start.15) | collective-permute-done | bytes 196640 | tf_op jit(solution)/shard_map/ppermute | solution.py:240
  75.5 5.6 %collective-permute-done.16.refs_3_ = bf16[16,6144]{1,0:T(8,128)(2,1)S(1)} collective-permute-done((bf16[16,6144]{1,0:T(8,128)(2,1)S(1)}, bf16[16,6144]{1,0:T(8,128)(2,1)S(1)}, u32[]{:S(2)}, u32[]{:S(2)}) %collective-permute-start.16) | collective-permute-done | bytes 196640 | tf_op jit(solution)/shard_map/ppermute | solution.py:240
  81.2 1.1 %shard_map.92 = bf16[16,12288]{1,0:T(8,128)(2,1)} custom-call(bf16[32,96]{1,0:T(8,128)(2,1)S(1)} %shard_map.90.plan_ref, bf16[16,6144]{1,0:T(8,128)(2,1)S(1)} %get-tuple-element.43.refs_0_, bf16[16,6144]{1,0:T(8,128)(2,1)S(1)} %collective-permute-done.14.refs_1_, bf16[16,6144]{1,0:T(8,128)(2,1)S(1)} %collective-permute-done.15.refs_2_, ...), custom_call_target="tpu_custom_call" | custom-call | bytes 1996800 | tf_op jit(solution)/shard_map/pallas_call | solution.py:218
  (36 shorter events, 1.1 us)
Async XLA Ops:
  2.4 4.0 %collective-permute-start.1 = (bf16[32,6272]{1,0:T(8,128)(2,1)}, bf16[32,6272]{1,0:T(8,128)(2,1)S(1)}, u32[]{:S(2)}, u32[]{:S(2)}) collective-permute-start(bf16[32,6272]{1,0:T(8,128)(2,1)} %shard_map.82.own_ids_ref.own_ref), channel_id=1, source_target_pairs={{0,1},{1,0},{2,3},{3,2},{4,5},{5,4},{6,7},{7,6},{8,9},{9,8},{10,11... | collective-permute-start | bytes 1204232 | tf_op jit(solution)/shard_map/ppermute | solution.py:240
  2.8 22.5 %collective-permute-start = (bf16[32,6272]{1,0:T(8,128)(2,1)}, bf16[32,6272]{1,0:T(8,128)(2,1)S(1)}, u32[]{:S(2)}, u32[]{:S(2)}) collective-permute-start(bf16[32,6272]{1,0:T(8,128)(2,1)} %shard_map.82.own_ids_ref.own_ref), channel_id=1, source_target_pairs={{0,8},{1,9},{2,10},{3,11},{4,12},{5,13},{6,14},{7,15},{8,0},{9,1},... | collective-permute-start | bytes 1204232 | tf_op jit(solution)/shard_map/ppermute | solution.py:240
  6.4 1.0 %copy-start = (bf16[32,6272]{1,0:T(8,128)(2,1)S(1)}, bf16[32,6272]{1,0:T(8,128)(2,1)}, u32[]{:S(2)}) copy-start(bf16[32,6272]{1,0:T(8,128)(2,1)} %shard_map.82.own_ids_ref.own_ref) | copy-start | bytes 1204228
  7.9 17.3 %collective-permute-start.2 = (bf16[16,6272]{1,0:T(8,128)(2,1)S(1)}, bf16[16,6272]{1,0:T(8,128)(2,1)S(1)}, u32[]{:S(2)}, u32[]{:S(2)}) collective-permute-start(bf16[16,6272]{1,0:T(8,128)(2,1)S(1)} %get-tuple-element.25), channel_id=1, source_target_pairs={{0,2},{1,3},{2,0},{3,1},{4,6},{5,7},{6,4},{7,5},{8,10},{9,11},{10,... | collective-permute-start | bytes 602120 | tf_op jit(solution)/shard_map/ppermute | solution.py:240
  9.5 15.8 %collective-permute-start.3 = (bf16[16,6272]{1,0:T(8,128)(2,1)S(1)}, bf16[16,6272]{1,0:T(8,128)(2,1)S(1)}, u32[]{:S(2)}, u32[]{:S(2)}) collective-permute-start(bf16[16,6272]{1,0:T(8,128)(2,1)S(1)} %get-tuple-element.26), channel_id=1, source_target_pairs={{0,4},{1,5},{2,6},{3,7},{4,0},{5,1},{6,2},{7,3},{8,12},{9,13},{10,... | collective-permute-start | bytes 602120 | tf_op jit(solution)/shard_map/ppermute | solution.py:240
  11.1 17.0 %collective-permute-start.4 = (bf16[16,6272]{1,0:T(8,128)(2,1)S(1)}, bf16[16,6272]{1,0:T(8,128)(2,1)S(1)}, u32[]{:S(2)}, u32[]{:S(2)}) collective-permute-start(bf16[16,6272]{1,0:T(8,128)(2,1)S(1)} %get-tuple-element.27), channel_id=1, source_target_pairs={{0,6},{1,7},{2,4},{3,5},{4,2},{5,3},{6,0},{7,1},{8,14},{9,15},{10,... | collective-permute-start | bytes 602120 | tf_op jit(solution)/shard_map/ppermute | solution.py:240
  28.1 14.9 %slice-start = ((s8[6291456]{0:T(1024)(128)(4,1)}), s8[4194304]{0:T(1024)(128)(4,1)S(1)}, s32[]{:S(2)}) async-start(s8[6291456]{0:T(1024)(128)(4,1)} %bitcast), calls=%async_computation | async-start | bytes 8388608
  28.1 14.9 %slice-start.2 = ((s8[6291456]{0:T(1024)(128)(4,1)}), s8[4194304]{0:T(1024)(128)(4,1)S(1)}, s32[]{:S(2)}) async-start(s8[6291456]{0:T(1024)(128)(4,1)} %bitcast.2), calls=%async_computation.2 | async-start | bytes 8388608
  28.1 14.9 %slice-start.1 = ((s8[6291456]{0:T(1024)(128)(4,1)}), s8[2097152]{0:T(1024)(128)(4,1)S(1)}, s32[]{:S(2)}) async-start(s8[6291456]{0:T(1024)(128)(4,1)} %bitcast), calls=%async_computation.1 | async-start | bytes 4194304
  28.1 14.9 %slice-start.3 = ((s8[6291456]{0:T(1024)(128)(4,1)}), s8[2097152]{0:T(1024)(128)(4,1)S(1)}, s32[]{:S(2)}) async-start(s8[6291456]{0:T(1024)(128)(4,1)} %bitcast.2), calls=%async_computation.3 | async-start | bytes 4194304
  28.1 14.9 %copy-start.4 = (bf16[256]{0:T(256)(128)(2,1)S(1)}, bf16[256]{0:T(256)(128)(2,1)}, u32[]{:S(2)}) copy-start(bf16[256]{0:T(256)(128)(2,1)} %refs_9_.1) | copy-start | bytes 1540
  28.1 1.8 %collective-permute-start.5 = (bf16[32,6272]{1,0:T(8,128)(2,1)S(1)}, bf16[32,6272]{1,0:T(8,128)(2,1)S(1)}, u32[]{:S(2)}, u32[]{:S(2)}) collective-permute-start(bf16[32,6272]{1,0:T(8,128)(2,1)S(1)} %shard_map.84.own_ids_ref.own_ref), channel_id=1, source_target_pairs={{0,1},{1,0},{2,3},{3,2},{4,5},{5,4},{6,7},{7,6},{8,9},{9,8},{10,11... | collective-permute-start | bytes 1204232 | tf_op jit(solution)/shard_map/ppermute | solution.py:240
  30.4 7.1 %collective-permute-start.6 = (bf16[16,6272]{1,0:T(8,128)(2,1)S(1)}, bf16[16,6272]{1,0:T(8,128)(2,1)S(1)}, u32[]{:S(2)}, u32[]{:S(2)}) collective-permute-start(bf16[16,6272]{1,0:T(8,128)(2,1)S(1)} %get-tuple-element.30), channel_id=1, source_target_pairs={{0,2},{1,3},{2,0},{3,1},{4,6},{5,7},{6,4},{7,5},{8,10},{9,11},{10,... | collective-permute-start | bytes 602120 | tf_op jit(solution)/shard_map/ppermute | solution.py:240
  32.0 7.9 %collective-permute-start.7 = (bf16[16,6272]{1,0:T(8,128)(2,1)S(1)}, bf16[16,6272]{1,0:T(8,128)(2,1)S(1)}, u32[]{:S(2)}, u32[]{:S(2)}) collective-permute-start(bf16[16,6272]{1,0:T(8,128)(2,1)S(1)} %get-tuple-element.31), channel_id=1, source_target_pairs={{0,4},{1,5},{2,6},{3,7},{4,0},{5,1},{6,2},{7,3},{8,12},{9,13},{10,... | collective-permute-start | bytes 602120 | tf_op jit(solution)/shard_map/ppermute | solution.py:240
  32.0 11.0 %collective-permute-start.8 = (bf16[16,6272]{1,0:T(8,128)(2,1)S(1)}, bf16[16,6272]{1,0:T(8,128)(2,1)S(1)}, u32[]{:S(2)}, u32[]{:S(2)}) collective-permute-start(bf16[16,6272]{1,0:T(8,128)(2,1)S(1)} %get-tuple-element.32), channel_id=1, source_target_pairs={{0,6},{1,7},{2,4},{3,5},{4,2},{5,3},{6,0},{7,1},{8,14},{9,15},{10,... | collective-permute-start | bytes 602120 | tf_op jit(solution)/shard_map/ppermute | solution.py:240
  45.1 20.3 %copy-start.3 = (s32[4,3]{1,0:T(4,128)S(1)}, s32[4,3]{1,0:T(4,128)}, u32[]{:S(2)}) copy-start(s32[4,3]{1,0:T(4,128)} %active_ref.3) | copy-start | bytes 148
  45.2 36.0 %copy-start.1 = (bf16[16,12288]{1,0:T(8,128)(2,1)S(1)}, bf16[16,12288]{1,0:T(8,128)(2,1)}, u32[]{:S(2)}) copy-start(bf16[16,12288]{1,0:T(8,128)(2,1)} %refs_5_.1) | copy-start | bytes 1179652
  45.2 36.0 %copy-start.2 = (bf16[12288]{0:T(1024)(128)(2,1)S(1)}, bf16[12288]{0:T(1024)(128)(2,1)}, u32[]{:S(2)}) copy-start(bf16[12288]{0:T(1024)(128)(2,1)} %refs_6_.1) | copy-start | bytes 73732
  45.2 7.0 %collective-permute-start.9 = (bf16[16,6144]{1,0:T(8,128)(2,1)S(1)}, bf16[16,6144]{1,0:T(8,128)(2,1)S(1)}, u32[]{:S(2)}, u32[]{:S(2)}) collective-permute-start(bf16[16,6144]{1,0:T(8,128)(2,1)S(1)} %get-tuple-element.34), channel_id=1, source_target_pairs={{0,2},{1,3},{2,0},{3,1},{4,6},{5,7},{6,4},{7,5},{8,10},{9,11},{10,... | collective-permute-start | bytes 589832 | tf_op jit(solution)/shard_map/ppermute | solution.py:240
  46.7 7.6 %collective-permute-start.10 = (bf16[16,6144]{1,0:T(8,128)(2,1)S(1)}, bf16[16,6144]{1,0:T(8,128)(2,1)S(1)}, u32[]{:S(2)}, u32[]{:S(2)}) collective-permute-start(bf16[16,6144]{1,0:T(8,128)(2,1)S(1)} %get-tuple-element.35), channel_id=1, source_target_pairs={{0,4},{1,5},{2,6},{3,7},{4,0},{5,1},{6,2},{7,3},{8,12},{9,13},{10,... | collective-permute-start | bytes 589832 | tf_op jit(solution)/shard_map/ppermute | solution.py:240
  47.0 9.4 %collective-permute-start.11 = (bf16[16,6144]{1,0:T(8,128)(2,1)S(1)}, bf16[16,6144]{1,0:T(8,128)(2,1)S(1)}, u32[]{:S(2)}, u32[]{:S(2)}) collective-permute-start(bf16[16,6144]{1,0:T(8,128)(2,1)S(1)} %get-tuple-element.36), channel_id=1, source_target_pairs={{0,6},{1,7},{2,4},{3,5},{4,2},{5,3},{6,0},{7,1},{8,14},{9,15},{10,... | collective-permute-start | bytes 589832 | tf_op jit(solution)/shard_map/ppermute | solution.py:240
  48.7 8.2 %collective-permute-start.13 = (bf16[32,6144]{1,0:T(8,128)(2,1)S(1)}, bf16[32,6144]{1,0:T(8,128)(2,1)S(1)}, u32[]{:S(2)}, u32[]{:S(2)}) collective-permute-start(bf16[32,6144]{1,0:T(8,128)(2,1)S(1)} %get-tuple-element.40), channel_id=1, source_target_pairs={{0,1},{1,0},{2,3},{3,2},{4,5},{5,4},{6,7},{7,6},{8,9},{9,8},{10,11... | collective-permute-start | bytes 1179656 | tf_op jit(solution)/shard_map/ppermute | solution.py:240
  56.9 1.8 %collective-permute-start.12 = (bf16[32,6144]{1,0:T(8,128)(2,1)S(1)}, bf16[32,6144]{1,0:T(8,128)(2,1)S(1)}, u32[]{:S(2)}, u32[]{:S(2)}) collective-permute-start(bf16[32,6144]{1,0:T(8,128)(2,1)S(1)} %get-tuple-element.38.refs_0_), channel_id=1, source_target_pairs={{0,1},{1,0},{2,3},{3,2},{4,5},{5,4},{6,7},{7,6},{8,9},{9,8},{10,11... | collective-permute-start | bytes 1179656 | tf_op jit(solution)/shard_map/ppermute | solution.py:240
  58.8 22.4 %collective-permute-start.17 = (bf16[32,6144]{1,0:T(8,128)(2,1)S(1)}, bf16[32,6144]{1,0:T(8,128)(2,1)S(1)}, u32[]{:S(2)}, u32[]{:S(2)}) collective-permute-start(bf16[32,6144]{1,0:T(8,128)(2,1)S(1)} %shard_map.89.order_ref.refs_0_), channel_id=1, source_target_pairs={{0,8},{1,9},{2,10},{3,11},{4,12},{5,13},{6,14},{7,15},{8,0},{9,1},... | collective-permute-start | bytes 1179656 | tf_op jit(solution)/shard_map/ppermute | solution.py:240
  61.8 13.7 %collective-permute-start.15 = (bf16[16,6144]{1,0:T(8,128)(2,1)S(1)}, bf16[16,6144]{1,0:T(8,128)(2,1)S(1)}, u32[]{:S(2)}, u32[]{:S(2)}) collective-permute-start(bf16[16,6144]{1,0:T(8,128)(2,1)S(1)} %get-tuple-element.41.refs_1_), channel_id=1, source_target_pairs={{0,4},{1,5},{2,6},{3,7},{4,0},{5,1},{6,2},{7,3},{8,12},{9,13},{10,... | collective-permute-start | bytes 589832 | tf_op jit(solution)/shard_map/ppermute | solution.py:240
  63.2 17.9 %collective-permute-start.16 = (bf16[16,6144]{1,0:T(8,128)(2,1)S(1)}, bf16[16,6144]{1,0:T(8,128)(2,1)S(1)}, u32[]{:S(2)}, u32[]{:S(2)}) collective-permute-start(bf16[16,6144]{1,0:T(8,128)(2,1)S(1)} %get-tuple-element.42.refs_2_), channel_id=1, source_target_pairs={{0,6},{1,7},{2,4},{3,5},{4,2},{5,3},{6,0},{7,1},{8,14},{9,15},{10,... | collective-permute-start | bytes 589832 | tf_op jit(solution)/shard_map/ppermute | solution.py:240
  64.8 16.3 %collective-permute-start.14 = (bf16[16,6144]{1,0:T(8,128)(2,1)S(1)}, bf16[16,6144]{1,0:T(8,128)(2,1)S(1)}, u32[]{:S(2)}, u32[]{:S(2)}) collective-permute-start(bf16[16,6144]{1,0:T(8,128)(2,1)S(1)} %get-tuple-element.44), channel_id=1, source_target_pairs={{0,2},{1,3},{2,0},{3,1},{4,6},{5,7},{6,4},{7,5},{8,10},{9,11},{10,... | collective-permute-start | bytes 589832 | tf_op jit(solution)/shard_map/ppermute | solution.py:240
